TPU v7x, 512 devices: a whole 4x8x8 slice. The times are simulated.
512 devices in a mesh: ch: 8 (over x, core), gx: 32 (over z, y_lo), gy: 2 (over y_hi).
Axes of the slice: x: 4, y: 8 (y_hi: 2, y_lo: 4; y = y_hi * 4 + y_lo), z: 8, core: 2. Of those that a mesh axis runs over, the one named last changes fastest.
Arguments:
- features: bfloat16 [128, 16, 2, 1024], P('gx', 'gy', None, 'ch'), may hold values from -6 to 6
- positions: float32 [3, 128, 16, 2], P(None, 'gx', 'gy'), may hold values from 0 to 1
- neighbours: int32 [128, 16, 2, 32], P('gx', 'gy'), may hold values from 0 to 17, as said below
- counts: int32 [128, 16, 2], P('gx', 'gy'), may hold values from 16 to 32
- species: int32 [128, 16, 2], P('gx', 'gy'), may hold values from 0 to 5
- radial_in: float32 [8, 64], replicated, may hold values from -2 to 2
- radial_out: bfloat16 [64, 3, 1024], P(None, None, 'ch'), may hold values from -0.75 to 0.75
- mix_weight: bfloat16 [3, 1024, 1024], P(None, None, 'ch'), may hold values from -0.1875 to 0.1875
- species_weight: float32 [6, 8, 1024], P(None, None, 'ch'), may hold values from -3 to 3
- out_weight: bfloat16 [1024, 1024], P(None, 'ch'), may hold values from -0.1875 to 0.1875
- readout: float32 [1024], P('ch'), may hold values from -0.1875 to 0.1875
Outputs:
- layer_out: bfloat16 [128, 16, 2, 1024], P('gx', 'gy', None, 'ch')
- energy: float32 [128, 16, 2], P('gx', 'gy')
- forces: float32 [3, 128, 16, 2], P(None, 'gx', 'gy')
- feature_grad: bfloat16 [128, 16, 2, 1024], P('gx', 'gy', None, 'ch')
- stress: float32 [3, 3], replicated
Inputs may be any that keep to these rules, and one draw needn't show every extreme that they name: `neighbours`: code ((dx + 1) * 3 + dy + 1) * 2 + slot names the atom in that slot of the cell column dx, dy columns away, periodically; never the atom itself.
All inputs are finite; a program needn't handle non-finite values.
Results may differ from a plain program's by a relative error of at most 0.012.
Values may be sent and summed in bfloat16 or wider, within the bound.
No kernel may reach another device: no remote copies, remote signals or barrier semaphores. Data moves between devices by JAX's collectives and lax.ppermute only.
A program may use at most 64 MiB of HBM per device.

v0:
```python
import math

import jax
import jax.numpy as jnp
from jax import lax
from jax.sharding import PartitionSpec as P

cutoff = 3.2
message_scale = 0.25
degree_bounds = ((0, 1), (1, 4), (4, 9))


def padded(block, sides, width):
    for axis, dim in sides:
        count = lax.axis_size(axis)
        forward = [(i, i + 1) for i in range(count - 1)]
        forward.append((count - 1, 0))
        backward = [(target, source) for source, target in forward]
        low = lax.ppermute(
            lax.slice_in_dim(block, block.shape[dim] - width, None, axis=dim), axis, forward
        )
        high = lax.ppermute(lax.slice_in_dim(block, 0, width, axis=dim), axis, backward)
        block = jnp.concatenate([low, block, high], axis=dim)
    return block


def from_behind(value, axis, by):
    peers = lax.axis_size(axis)
    return lax.ppermute(value, axis, [(i, (i + by) % peers) for i in range(peers)])


def geometry(offsets, radial_in):
    squared = jnp.sum(offsets * offsets, axis=0) + 0.25
    distance = jnp.sqrt(squared)
    unit_x = offsets[0] / distance
    unit_y = offsets[1] / distance
    unit_z = offsets[2] / distance
    harmonic = jnp.stack(
        [
            jnp.ones_like(unit_x),
            unit_x,
            unit_y,
            unit_z,
            unit_x * unit_y,
            unit_y * unit_z,
            1.5 * unit_z * unit_z - 0.5,
            unit_x * unit_z,
            0.5 * (unit_x * unit_x - unit_y * unit_y),
        ]
    )
    ratio = distance / cutoff
    envelope = (1.0 - ratio * ratio) ** 2
    orders = jnp.arange(1, radial_in.shape[0] + 1).astype(jnp.float32)
    basis = jnp.sin(math.pi * orders[:, None] * ratio[None, :]) * (envelope / distance)[None, :]
    hidden = jax.nn.silu(jnp.einsum("be,bh->eh", basis, radial_in, precision=lax.Precision.HIGHEST))
    return (harmonic, hidden)


def contract(mixed, chosen):
    center = mixed[:, 0]
    vec_x = mixed[:, 1]
    vec_y = mixed[:, 2]
    vec_z = mixed[:, 3]
    quad_a = mixed[:, 4]
    quad_b = mixed[:, 5]
    quad_c = mixed[:, 6]
    quad_d = mixed[:, 7]
    quad_e = mixed[:, 8]
    vec_sq = vec_x * vec_x + vec_y * vec_y + vec_z * vec_z
    quad_sq = (
        quad_a * quad_a + quad_b * quad_b + quad_c * quad_c + quad_d * quad_d + quad_e * quad_e
    )
    cubic = (
        (quad_e - quad_c) * vec_x * vec_x
        - (quad_e + quad_c) * vec_y * vec_y
        + 2.0 * quad_c * vec_z * vec_z
        + 2.0 * (quad_a * vec_x * vec_y + quad_b * vec_y * vec_z + quad_d * vec_x * vec_z)
    )
    terms = jnp.stack(
        [
            center,
            center * center,
            vec_sq,
            quad_sq,
            center * center * center,
            center * vec_sq,
            center * quad_sq,
            cubic,
        ],
        axis=1,
    )
    return jnp.sum(terms * chosen, axis=1)


def body(
    features,
    positions,
    neighbours,
    counts,
    species,
    radial_in,
    radial_out,
    mix_weight,
    species_weight,
    out_weight,
    readout,
):
    cells_x, cells_y, slot_count, chan_dev = features.shape
    neigh_count = neighbours.shape[-1]
    atom_count = cells_x * cells_y * slot_count
    edge_count = atom_count * neigh_count
    ext_feat = padded(features, (("gx", 0), ("gy", 1)), 1)
    ext_pos = padded(positions, (("gx", 1), ("gy", 2)), 1)
    codes = neighbours.reshape(atom_count, neigh_count)
    step_x = codes // (3 * slot_count) - 1
    step_y = codes // slot_count % 3 - 1
    slot_nb = codes % slot_count
    local = jnp.arange(atom_count, dtype=jnp.int32)
    own_x = (local // (cells_y * slot_count))[:, None]
    own_y = (local // slot_count % cells_y)[:, None]
    where_ext = (
        ((own_x + 1 + step_x) * (cells_y + 2) + own_y + 1 + step_y) * slot_count + slot_nb
    ).reshape(-1)
    pos_nb = ext_pos.reshape(3, -1)[:, where_ext].reshape(3, atom_count, neigh_count)
    pos_own = positions.reshape(3, atom_count)
    offsets = jnp.stack(
        [
            step_x.astype(jnp.float32) + pos_nb[0] - pos_own[0][:, None],
            step_y.astype(jnp.float32) + pos_nb[1] - pos_own[1][:, None],
            pos_nb[2] - pos_own[2][:, None],
        ]
    ).reshape(3, edge_count)
    live = (
        jnp.arange(neigh_count, dtype=jnp.int32)[None, :] < counts.reshape(atom_count, 1)
    ).astype(jnp.float32)
    (harmonic, hidden), geo_back = jax.vjp(lambda values: geometry(values, radial_in), offsets)
    harm_live = (harmonic.reshape(9, atom_count, neigh_count) * live[None]).transpose(1, 2, 0)
    hidden_bf = hidden.astype(jnp.bfloat16)
    nb_feat = ext_feat.reshape(-1, chan_dev)[where_ext].reshape(atom_count, neigh_count, chan_dev)
    radials = []
    message_parts = []
    for degree, (first, last) in enumerate(degree_bounds):
        radial = jnp.dot(hidden_bf, radial_out[:, degree, :], preferred_element_type=jnp.float32)
        radial = radial.reshape(atom_count, neigh_count, chan_dev)
        radials.append(radial)
        product = radial * nb_feat
        message_parts.append(
            message_scale
            * jnp.einsum(
                "anm,ank->amk",
                harm_live[:, :, first:last],
                product,
                precision=lax.Precision.HIGHEST,
            )
        )
    message = jnp.concatenate(message_parts, axis=1).astype(jnp.bfloat16)
    piece = lax.all_gather(message, "ch", axis=2, tiled=True)
    width = piece.shape[2]
    parts = []
    for mix_degree, (mix_first, mix_last) in enumerate(degree_bounds):
        weight_rows = mix_weight[mix_degree]
        block = piece[:, mix_first:mix_last, :].reshape(-1, width)
        parts.append(
            jnp.dot(block, weight_rows, preferred_element_type=jnp.float32).reshape(
                atom_count, mix_last - mix_first, chan_dev
            )
        )
    mixed = jnp.concatenate(parts, axis=1)
    onehot = (
        species.reshape(atom_count, 1)
        == jnp.arange(species_weight.shape[0], dtype=jnp.int32)[None, :]
    ).astype(jnp.float32)
    chosen = jnp.einsum("as,stk->atk", onehot, species_weight, precision=lax.Precision.HIGHEST)
    products = contract(mixed, chosen).astype(jnp.bfloat16)
    weight_rows = out_weight
    layer = jnp.dot(
        lax.all_gather(products, "ch", axis=1, tiled=True),
        weight_rows,
        preferred_element_type=jnp.float32,
    )
    layer = layer + features.reshape(atom_count, chan_dev).astype(jnp.float32)
    energy_part = jnp.sum(layer * readout[None, :], axis=1)
    vector_part = jnp.dot(out_weight.astype(jnp.float32), readout, precision=lax.Precision.HIGHEST)
    energy = lax.psum(energy_part, "ch")
    vector = lax.psum_scatter(vector_part, "ch", scatter_dimension=0, tiled=True)
    cotangent = jnp.broadcast_to(vector[None, :], (atom_count, chan_dev))
    dummy, pullback = jax.vjp(lambda values: contract(values, chosen), mixed)
    adjoint_bf = pullback(cotangent)[0].astype(jnp.bfloat16)
    own_start = lax.axis_index("ch") * chan_dev
    rows_own = lax.dynamic_slice_in_dim(
        lax.all_gather(mix_weight, "ch", axis=2, tiled=True), own_start, chan_dev, 1
    )
    piece = lax.all_gather(adjoint_bf, "ch", axis=2, tiled=True)
    width = piece.shape[2]
    parts = []
    for back_degree, (back_first, back_last) in enumerate(degree_bounds):
        weight_cols = rows_own[back_degree]
        block = piece[:, back_first:back_last, :].reshape(-1, width)
        parts.append(
            lax.dot_general(
                block, weight_cols, (((1,), (1,)), ((), ())), preferred_element_type=jnp.float32
            ).reshape(atom_count, back_last - back_first, chan_dev)
        )
    adjoint_message = jnp.concatenate(parts, axis=1)
    harm_grads = []
    feature_back = jnp.zeros((atom_count, neigh_count, chan_dev), jnp.float32)
    grad_hidden = jnp.zeros((edge_count, radial_out.shape[0]), jnp.float32)
    for degree, (first, last) in enumerate(degree_bounds):
        grad_slice = adjoint_message[:, first:last, :]
        grad_prod = message_scale * jnp.einsum(
            "anm,amk->ank", harm_live[:, :, first:last], grad_slice, precision=lax.Precision.HIGHEST
        )
        product = radials[degree] * nb_feat
        harm_grads.append(
            message_scale
            * jnp.einsum("amk,ank->anm", grad_slice, product, precision=lax.Precision.HIGHEST)
        )
        grad_radial = (grad_prod * nb_feat).reshape(edge_count, chan_dev).astype(jnp.bfloat16)
        feature_back = feature_back + grad_prod * radials[degree]
        grad_hidden = grad_hidden + lax.dot_general(
            grad_radial,
            radial_out[:, degree, :],
            (((1,), (1,)), ((), ())),
            preferred_element_type=jnp.float32,
        )
    harm_grad = (
        (jnp.concatenate(harm_grads, axis=2) * live[:, :, None])
        .transpose(2, 0, 1)
        .reshape(9, edge_count)
    )
    harm_total, hidden_total = lax.psum((harm_grad, grad_hidden), "ch")
    edge_grad = geo_back((harm_total, hidden_total))[0]
    own_force = jnp.sum(edge_grad.reshape(3, atom_count, neigh_count), axis=2)
    ext_cells = (cells_x + 2) * (cells_y + 2) * slot_count
    grid_force = jnp.zeros((3, ext_cells), jnp.float32).at[:, where_ext].add(-edge_grad)
    grid_force = grid_force.reshape(3, cells_x + 2, cells_y + 2, slot_count)
    grid_feat = (
        jnp.zeros((ext_cells, chan_dev), jnp.float32)
        .at[where_ext]
        .add(feature_back.reshape(edge_count, chan_dev))
    )
    grid_feat = grid_feat.reshape(cells_x + 2, cells_y + 2, slot_count, chan_dev)
    for shift_by in (1, -1):
        send_row = cells_x + 1 if shift_by == 1 else 0
        land_row = 1 if shift_by == 1 else cells_x
        payload = jnp.concatenate(
            [grid_feat[send_row].reshape(-1), grid_force[:, send_row].reshape(-1)]
        )
        arrived = from_behind(payload, "gx", shift_by)
        feat_size = (cells_y + 2) * slot_count * chan_dev
        grid_feat = grid_feat.at[land_row].add(
            arrived[:feat_size].reshape(cells_y + 2, slot_count, chan_dev)
        )
        grid_force = grid_force.at[:, land_row].add(
            arrived[feat_size:].reshape(3, cells_y + 2, slot_count)
        )
    inner_feat = grid_feat[1 : cells_x + 1]
    inner_force = grid_force[:, 1 : cells_x + 1]
    for shift_by in (1, -1):
        send_col = cells_y + 1 if shift_by == 1 else 0
        land_col = 1 if shift_by == 1 else cells_y
        payload = jnp.concatenate(
            [inner_feat[:, send_col].reshape(-1), inner_force[:, :, send_col].reshape(-1)]
        )
        arrived = from_behind(payload, "gy", shift_by)
        feat_size = cells_x * slot_count * chan_dev
        inner_feat = inner_feat.at[:, land_col].add(
            arrived[:feat_size].reshape(cells_x, slot_count, chan_dev)
        )
        inner_force = inner_force.at[:, :, land_col].add(
            arrived[feat_size:].reshape(3, cells_x, slot_count)
        )
    feature_grad = (inner_feat[:, 1 : cells_y + 1] + readout).astype(jnp.bfloat16)
    forces = own_force.reshape(3, cells_x, cells_y, slot_count) + inner_force[:, :, 1 : cells_y + 1]
    total_atoms = atom_count * lax.axis_size("gx") * lax.axis_size("gy")
    virial_part = (
        jnp.einsum("ae,be->ab", offsets, edge_grad, precision=lax.Precision.HIGHEST) / total_atoms
    )
    stress = lax.psum(virial_part, ("gx", "gy"))
    layer_out = layer.astype(jnp.bfloat16).reshape(cells_x, cells_y, slot_count, chan_dev)
    return (layer_out, energy.reshape(cells_x, cells_y, slot_count), forces, feature_grad, stress)


def solution(mesh):
    placed = (
        P("gx", "gy", None, "ch"),
        P(None, "gx", "gy", None),
        P("gx", "gy", None, None),
        P("gx", "gy", None),
        P("gx", "gy", None),
        P(),
        P(None, None, "ch"),
        P(None, None, "ch"),
        P(None, None, "ch"),
        P(None, "ch"),
        P("ch"),
    )
    return jax.shard_map(
        body,
        mesh=mesh,
        in_specs=placed,
        out_specs=(
            P("gx", "gy", None, "ch"),
            P("gx", "gy", None),
            P(None, "gx", "gy", None),
            P("gx", "gy", None, "ch"),
            P(),
        ),
        check_vma=False,
    )
```

profile of v0, /device:TPU:8, one launch (start us, length us, event | category | flops | bytes accessed | tf_op | source)
XLA Modules:
  0.0 568.2 jit_solution(12181030268012616668)
XLA Ops:
  8.0 3.5 collective-permute-start
  11.4 6.2 %collective-permute-start.1 = (f32[3,1,8,2]{2,3,1,0:T(2,128)S(1)}, f32[3,1,8,2]{2,3,1,0:T(2,128)S(1)}, u32[]{:S(2)}, u32[]{:S(2)}) collective-permute-start(f32[3,1,8,2]{2,3,1,0:T(2,128)S(1)} %get-tuple-element.211), channel_id=1, source_target_pairs={{2,0},{4,2},{6,4},{8,6},{10,8},{12,10},{14,12},{16,14},{18,16},{20... | collective-permute-start | bytes 584 | tf_op jit(solution)/shard_map/ppermute | solution.py:22
  17.6 1.3 fusion.195
  18.9 1.9 collective-permute-start.4
  20.8 8.6 %collective-permute-start.5 = (bf16[1,8,2,128]{3,2,1,0:T(2,128)(2,1)}, bf16[1,8,2,128]{3,2,1,0:T(2,128)(2,1)}, u32[]{:S(2)}, u32[]{:S(2)}) collective-permute-start(bf16[1,8,2,128]{3,2,1,0:T(2,128)(2,1)} %get-tuple-element.206), channel_id=1, source_target_pairs={{2,0},{4,2},{6,4},{8,6},{10,8},{12,10},{14,12},{16,14},{18,16},{20... | collective-permute-start | bytes 12296 | tf_op jit(solution)/shard_map/ppermute | solution.py:22
  30.2 0.9 reshape.1024
  31.1 0.9 reshape.1022
  33.6 0.8 copy.272
  35.7 5.0 collective-permute-start.3
  40.8 4.7 collective-permute-start.2
  45.6 4.7 collective-permute-done.2
  50.6 5.5 gather_fusion
  57.3 1.6 multiply_convert_fusion
  59.2 1.3 fusion.106
  64.3 4.7 collective-permute-start.7
  69.0 5.0 collective-permute-start.6
  74.1 4.3 collective-permute-done.6
  78.5 6.2 %gather_fusion.1 = bf16[2048,128]{1,0:T(8,128)(2,1)S(1)} fusion(bf16[120,128]{1,0:T(8,128)(2,1)S(1)} %bitcast.471, s32[2048]{0:T(1024)S(1)} %broadcast_clamp_fusion), kind=kCustom, calls=%fused_computation.1 | custom fusion | bytes 1056768 | tf_op jit(solution)/shard_map/gather | solution.py:139
  84.6 2.2 fusion
  86.9 1.0 fusion.1
  87.9 1.0 fusion.6
  89.0 0.9 pad_maximum_fusion
  90.7 1.3 dynamic-slice.56
  92.6 0.9 fusion.177
  93.5 32.9 %all-gather.4.cloned.1.call-done = bf16[64,9,1024]{2,1,0:T(8,128)(2,1)} async-done(((bf16[64,9,128]{2,1,0:T(8,128)(2,1)}), bf16[64,9,1024]{2,1,0:T(8,128)(2,1)}) %all-gather.4.cloned.1.call-update) | async-done | bytes 1179664 | tf_op jit(solution)/shard_map/all_gather | solution.py:157
  126.5 1.5 slice.542
  128.0 1.3 bitcast_dynamic-update-slice_fusion.2
  129.2 1.5 slice.543
  131.5 0.8 fusion.7
  133.1 1.1 multiply_reduce_fusion
  134.2 11.6 %all_gather.13 = bf16[64,1024]{1,0:T(8,128)(2,1)S(1)} all-gather(bf16[64,128]{1,0:T(8,128)(2,1)S(1)} %get-tuple-element.221), channel_id=1, replica_groups=mesh['ch'=8,'gx'=32,'gy'=2] {'ch'}, dimensions={1}, use_global_device_ids=true | all-gather | bytes 147456 | tf_op jit(solution)/shard_map/all_gather | solution.py:177
  145.8 1.4 multiply_reduce_fusion.1
  148.0 26.1 %all-reduce.13 = (f32[4,8,2]{2,1,0:T(8,128)}, f32[1024]{0:T(1024)}) all-reduce(f32[4,8,2]{2,1,0:T(8,128)S(1)} %reshape.1030, f32[1024]{0:T(1024)} %bitcast.524), channel_id=1, replica_groups=mesh['ch'=8,'gx'=32,'gy'=2] {'ch'}, use_global_device_ids=true, to_apply=%region_3.4 | all-reduce | flops 1088 | bytes 8704 | tf_op jit(solution)/shard_map/psum | solution.py:184
  174.1 0.8 dynamic-slice.57
  174.8 1.0 broadcast_multiply_fusion
  175.8 0.9 fusion.59
  176.7 0.8 fusion.62
  180.6 25.9 %all-gather.6.cloned.1.call-done = bf16[64,9,1024]{2,0,1:T(8,128)(2,1)} async-done(((bf16[64,9,128]{2,0,1:T(8,128)(2,1)}), bf16[64,9,1024]{2,0,1:T(8,128)(2,1)}) %all-gather.6.cloned.1.call-update) | async-done | bytes 1179664 | tf_op jit(solution)/shard_map/all_gather | solution.py:193
  206.4 53.5 %all-gather.8.cloned.1.call-done = bf16[3,1024,1024]{2,1,0:T(8,128)(2,1)} async-done(((bf16[3,1024,128]{2,1,0:T(8,128)(2,1)}), bf16[3,1024,1024]{2,1,0:T(8,128)(2,1)}) %all-gather.8.cloned.1.call-update) | async-done | bytes 6291472 | tf_op jit(solution)/shard_map/all_gather | solution.py:191
  259.9 1.3 fusion.19
  261.3 1.8 convolution_multiply_fusion.4
  263.0 2.8 convolution_multiply_fusion
  265.8 1.3 fusion.18
  267.8 2.5 convolution_multiply_fusion.2
  270.3 1.7 copy.282
  272.7 1.2 fusion.20
  274.6 1.7 fusion.5
  276.4 0.9 fusion.31
  277.3 0.9 copy.284
  278.2 1.8 reshape.1032
  279.9 4.9 multiply_add_fusion
  285.5 1.1 convolution_add_fusion
  287.0 12.1 %scatter_custom_fusion.1 = f32[120,128]{1,0:T(8,128)S(1)} fusion(s32[2048]{0:T(1024)} %bitcast.517, f32[2048,128]{1,0:T(8,128)} %bitcast.486, f32[]{:T(128)} %constant.331.clone.1), kind=kCustom, calls=%fused_computation.222 | custom fusion | flops 262144 | bytes 61952 | tf_op jit(solution)/shard_map/scatter-add | solution.py:240
  299.0 60.8 %all-reduce.17.cloned.1.call-done = (f32[9,2048]{1,0:T(8,128)}, f32[2048,64]{0,1:T(8,128)}) async-done(((f32[9,2048]{1,0:T(8,128)}, f32[2048,64]{0,1:T(8,128)}), (f32[9,2048]{1,0:T(8,128)}, f32[2048,64]{0,1:T(8,128)})) %all-reduce.17.cloned.1.call-update) | async-done | bytes 598032 | tf_op jit(solution)/shard_map/psum | solution.py:231
  359.9 1.1 fusion.190
  361.1 1.9 fusion.42
  363.7 11.6 %scatter_custom_fusion = f32[3,120]{0,1:T(8,128)S(1)} fusion(s32[2048]{0:T(1024)} %bitcast.518, f32[2048,3]{1,0:T(8,128)S(1)} %copy.289, f32[]{:T(128)} %constant.331.clone.1), kind=kCustom, calls=%fused_computation.224 | custom fusion | flops 6144 | bytes 1952 | tf_op jit(solution)/shard_map/scatter-add | solution.py:235
  375.6 3.4 collective-permute-start.8
  379.8 1.4 collective-permute-done.8
  381.6 7.2 %collective-permute-start.9 = (f32[2620]{0:T(1024)S(1)}, f32[2620]{0:T(1024)S(1)}, u32[]{:S(2)}, u32[]{:S(2)}) collective-permute-start(f32[2620]{0:T(1024)S(1)} %pad_maximum_fusion.5), channel_id=1, source_target_pairs={{0,62},{2,0},{4,2},{6,4},{8,6},{10,8},{12,10},{14,12},{16,14},{18,... | collective-permute-start | bytes 31448 | tf_op jit(solution)/shard_map/ppermute | solution.py:29
  390.4 6.6 %collective-permute-start.10 = (f32[1048]{0:T(1024)S(1)}, f32[1048]{0:T(1024)S(1)}, u32[]{:S(2)}, u32[]{:S(2)}) collective-permute-start(f32[1048]{0:T(1024)S(1)} %pad_maximum_fusion.6), channel_id=1, source_target_pairs={{0,1},{1,0},{2,3},{3,2},{4,5},{5,4},{6,7},{7,6},{8,9},{9,8},{10,11... | collective-permute-start | bytes 12584 | tf_op jit(solution)/shard_map/ppermute | solution.py:29
  397.6 2.2 collective-permute-done.10
  400.2 6.6 %collective-permute-start.11 = (f32[1048]{0:T(1024)S(1)}, f32[1048]{0:T(1024)S(1)}, u32[]{:S(2)}, u32[]{:S(2)}) collective-permute-start(f32[1048]{0:T(1024)S(1)} %pad_maximum_fusion.7), channel_id=1, source_target_pairs={{0,1},{1,0},{2,3},{3,2},{4,5},{5,4},{6,7},{7,6},{8,9},{9,8},{10,11... | collective-permute-start | bytes 12584 | tf_op jit(solution)/shard_map/ppermute | solution.py:29
  407.0 152.9 %psum.31 = f32[3,3]{1,0:T(4,128)} all-reduce(f32[3,3]{1,0:T(4,128)S(1)} %convolution_multiply_fusion.6), channel_id=1, replica_groups=mesh['ch'=8,'gx'=32,'gy'=2] {'gx','gy'}, use_global_device_ids=true, to_apply=%region_12.13 | all-reduce | flops 9 | bytes 72 | tf_op jit(solution)/shard_map/psum | solution.py:279
  (270 shorter events, 25.7 us)
Async XLA Ops:
  7.2 85.4 %copy-start = (bf16[1024,128]{1,0:T(8,128)(2,1)S(1)}, bf16[1024,128]{1,0:T(8,128)(2,1)}, u32[]{:S(2)}) copy-start(bf16[1024,128]{1,0:T(8,128)(2,1)} %param.36) | copy-start | bytes 786436
  7.2 119.3 %all-gather.4.cloned.1.call-start = ((), (), s32[]{:S(2)}) async-start(), calls=%async_computation | async-start | bytes 2359296 | tf_op jit(solution)/shard_map/all_gather | solution.py:157
  8.0 26.9 %collective-permute-start = (f32[3,1,8,2]{2,3,1,0:T(2,128)S(1)}, f32[3,1,8,2]{2,3,1,0:T(2,128)S(1)}, u32[]{:S(2)}, u32[]{:S(2)}) collective-permute-start(f32[3,1,8,2]{2,3,1,0:T(2,128)S(1)} %get-tuple-element.212), channel_id=1, source_target_pairs={{0,2},{2,4},{4,6},{6,8},{8,10},{10,12},{12,14},{14,16},{16,18},{18... | collective-permute-start | bytes 584 | tf_op jit(solution)/shard_map/ppermute | solution.py:19
  11.4 24.2 %collective-permute-start.1 = (f32[3,1,8,2]{2,3,1,0:T(2,128)S(1)}, f32[3,1,8,2]{2,3,1,0:T(2,128)S(1)}, u32[]{:S(2)}, u32[]{:S(2)}) collective-permute-start(f32[3,1,8,2]{2,3,1,0:T(2,128)S(1)} %get-tuple-element.211), channel_id=1, source_target_pairs={{2,0},{4,2},{6,4},{8,6},{10,8},{12,10},{14,12},{16,14},{18,16},{20... | collective-permute-start | bytes 584 | tf_op jit(solution)/shard_map/ppermute | solution.py:22
  18.9 43.9 %collective-permute-start.4 = (bf16[1,8,2,128]{3,2,1,0:T(2,128)(2,1)}, bf16[1,8,2,128]{3,2,1,0:T(2,128)(2,1)}, u32[]{:S(2)}, u32[]{:S(2)}) collective-permute-start(bf16[1,8,2,128]{3,2,1,0:T(2,128)(2,1)} %get-tuple-element.207), channel_id=1, source_target_pairs={{0,2},{2,4},{4,6},{6,8},{8,10},{10,12},{12,14},{14,16},{16,18},{18... | collective-permute-start | bytes 12296 | tf_op jit(solution)/shard_map/ppermute | solution.py:19
  20.8 42.7 %collective-permute-start.5 = (bf16[1,8,2,128]{3,2,1,0:T(2,128)(2,1)}, bf16[1,8,2,128]{3,2,1,0:T(2,128)(2,1)}, u32[]{:S(2)}, u32[]{:S(2)}) collective-permute-start(bf16[1,8,2,128]{3,2,1,0:T(2,128)(2,1)} %get-tuple-element.206), channel_id=1, source_target_pairs={{2,0},{4,2},{6,4},{8,6},{10,8},{12,10},{14,12},{16,14},{18,16},{20... | collective-permute-start | bytes 12296 | tf_op jit(solution)/shard_map/ppermute | solution.py:22
  31.9 25.3 %copy-start.52 = (f32[8]{0:T(128)}, f32[8]{0:T(128)S(1)}, u32[]{:S(2)}) copy-start(f32[8]{0:T(128)S(1)} %convert_multiply_fusion.12) | copy-start | bytes 100
  32.4 2.2 copy-start.36
  32.9 24.3 %copy-start.50 = (f32[8,64]{1,0:T(8,128)S(1)}, f32[8,64]{1,0:T(8,128)}, u32[]{:S(2)}) copy-start(f32[8,64]{1,0:T(8,128)} %param.32) | copy-start | bytes 6148
  34.5 39.5 %copy-start.16 = (f32[64,32]{1,0:T(8,128)}, f32[64,32]{1,0:T(8,128)S(1)}, u32[]{:S(2)}) copy-start(f32[64,32]{1,0:T(8,128)S(1)} %fusion.97) | copy-start | bytes 24580
  34.6 15.7 %copy-start.10 = (f32[64,32]{1,0:T(8,128)}, f32[64,32]{1,0:T(8,128)S(1)}, u32[]{:S(2)}) copy-start(f32[64,32]{1,0:T(8,128)S(1)} %sub.195) | copy-start | bytes 24580
  34.8 15.5 %copy-start.12 = (f32[64,32]{1,0:T(8,128)}, f32[64,32]{1,0:T(8,128)S(1)}, u32[]{:S(2)}) copy-start(f32[64,32]{1,0:T(8,128)S(1)} %sub.176) | copy-start | bytes 24580
  35.7 9.9 %collective-permute-start.3 = (f32[3,6,1,2]{2,3,1,0:T(2,128)S(1)}, f32[3,6,1,2]{2,3,1,0:T(2,128)S(1)}, u32[]{:S(2)}, u32[]{:S(2)}) collective-permute-start(f32[3,6,1,2]{2,3,1,0:T(2,128)S(1)} %get-tuple-element.205), channel_id=1, source_target_pairs={{1,0},{0,1},{3,2},{2,3},{5,4},{4,5},{7,6},{6,7},{9,8},{8,9},{11,10... | collective-permute-start | bytes 440 | tf_op jit(solution)/shard_map/ppermute | solution.py:22
  40.8 9.6 %collective-permute-start.2 = (f32[3,6,1,2]{2,3,1,0:T(2,128)S(1)}, f32[3,6,1,2]{2,3,1,0:T(2,128)S(1)}, u32[]{:S(2)}, u32[]{:S(2)}) collective-permute-start(f32[3,6,1,2]{2,3,1,0:T(2,128)S(1)} %get-tuple-element.204), channel_id=1, source_target_pairs={{0,1},{1,0},{2,3},{3,2},{4,5},{5,4},{6,7},{7,6},{8,9},{9,8},{10,11... | collective-permute-start | bytes 440 | tf_op jit(solution)/shard_map/ppermute | solution.py:19
  45.5 5.1 copy-start.14
  57.1 1.8 copy-start.26
  57.1 1.8 copy-start.28
  57.1 1.8 copy-start.30
  57.2 1.7 copy-start.24
  57.2 1.7 copy-start.41
  57.2 1.7 copy-start.43
  57.2 3.9 copy-start.22
  57.3 2.0 copy-start.18
  60.8 2.7 copy-start.20
  64.3 9.8 %collective-permute-start.7 = (bf16[6,1,2,128]{3,2,1,0:T(2,128)(2,1)S(1)}, bf16[6,1,2,128]{3,2,1,0:T(2,128)(2,1)S(1)}, u32[]{:S(2)}, u32[]{:S(2)}) collective-permute-start(bf16[6,1,2,128]{3,2,1,0:T(2,128)(2,1)S(1)} %get-tuple-element.203), channel_id=1, source_target_pairs={{1,0},{0,1},{3,2},{2,3},{5,4},{4,5},{7,6},{6,7},{9,8},{8,9},{11,10... | collective-permute-start | bytes 9224 | tf_op jit(solution)/shard_map/ppermute | solution.py:22
  69.0 9.4 %collective-permute-start.6 = (bf16[6,1,2,128]{3,2,1,0:T(2,128)(2,1)S(1)}, bf16[6,1,2,128]{3,2,1,0:T(2,128)(2,1)S(1)}, u32[]{:S(2)}, u32[]{:S(2)}) collective-permute-start(bf16[6,1,2,128]{3,2,1,0:T(2,128)(2,1)S(1)} %get-tuple-element.202), channel_id=1, source_target_pairs={{0,1},{1,0},{2,3},{3,2},{4,5},{5,4},{6,7},{7,6},{8,9},{9,8},{10,11... | collective-permute-start | bytes 9224 | tf_op jit(solution)/shard_map/ppermute | solution.py:19
  87.9 2.1 copy-start.48
  87.9 4.7 copy-start.45
  89.9 116.5 %all-gather.6.cloned.1.call-start = ((), (), s32[]{:S(2)}) async-start(), calls=%async_computation.1 | async-start | bytes 1327104 | tf_op jit(solution)/shard_map/all_gather | solution.py:193
  126.5 4.3 copy-start.7
  128.0 3.1 copy-start.6
  131.5 1.6 copy-start.32
  131.5 1.6 copy-start.49
  132.3 13.5 %copy-start.46 = (f32[128]{0:T(128)S(1)}, f32[128]{0:T(128)}, u32[]{:S(2)}) copy-start(f32[128]{0:T(128)} %param.37) | copy-start | bytes 1540
  174.0 3.4 copy-start.3
  177.5 1.8 copy-start.17
  178.3 81.6 %all-gather.8.cloned.1.call-start = ((), (), s32[]{:S(2)}) async-start(), calls=%async_computation.2 | async-start | bytes 7077888 | tf_op jit(solution)/shard_map/all_gather | solution.py:191
  179.0 180.8 %all-reduce.17.cloned.1.call-start = ((), (), s32[]{:S(2)}) async-start(), calls=%async_computation.3 | async-start | bytes 1310720 | tf_op jit(solution)/shard_map/psum | solution.py:231
  261.2 4.6 copy-start.5
  263.0 4.8 copy-start.1
  279.9 4.9 copy-start.19
  285.5 75.5 %copy-start.42 = (f32[2048]{0:T(1024)S(1)}, f32[2048]{0:T(1024)}, u32[]{:S(2)}) copy-start(f32[2048]{0:T(1024)} %copy-done.41) | copy-start | bytes 24580
  285.5 75.5 %copy-start.44 = (f32[2048]{0:T(1024)S(1)}, f32[2048]{0:T(1024)}, u32[]{:S(2)}) copy-start(f32[2048]{0:T(1024)} %copy-done.43) | copy-start | bytes 24580
  285.5 75.5 %copy-start.51 = (f32[8,64]{1,0:T(8,128)S(1)}, f32[8,64]{1,0:T(8,128)}, u32[]{:S(2)}) copy-start(f32[8,64]{1,0:T(8,128)} %param.32) | copy-start | bytes 6148
  285.5 75.5 %copy-start.53 = (f32[8]{0:T(128)S(1)}, f32[8]{0:T(128)}, u32[]{:S(2)}) copy-start(f32[8]{0:T(128)} %copy-done.52) | copy-start | bytes 100
  285.5 75.5 %copy-start.54 = (f32[2048,64]{0,1:T(8,128)S(1)}, f32[2048,64]{0,1:T(8,128)}, u32[]{:S(2)}) copy-start(f32[2048,64]{0,1:T(8,128)} %get-tuple-element.218) | copy-start | bytes 1572868
  361.0 2.0 copy-start.21
  361.0 2.0 copy-start.23
  361.0 2.0 copy-start.33
  361.0 2.0 copy-start.34
  361.0 2.0 copy-start.35
  361.0 2.1 copy-start.25
  361.1 2.1 copy-start.37
  361.1 2.1 copy-start.38
  361.1 2.1 copy-start.39
  361.1 2.2 copy-start.27
  361.1 2.2 copy-start.29
  361.1 2.2 copy-start.31
  363.0 25.7 %copy-start.40 = (f32[4,8,2]{2,1,0:T(8,128)S(1)}, f32[4,8,2]{2,1,0:T(8,128)}, u32[]{:S(2)}) copy-start(f32[4,8,2]{2,1,0:T(8,128)} %get-tuple-element.141) | copy-start | bytes 772
  375.6 5.6 collective-permute-start.8
  381.6 8.5 %collective-permute-start.9 = (f32[2620]{0:T(1024)S(1)}, f32[2620]{0:T(1024)S(1)}, u32[]{:S(2)}, u32[]{:S(2)}) collective-permute-start(f32[2620]{0:T(1024)S(1)} %pad_maximum_fusion.5), channel_id=1, source_target_pairs={{0,62},{2,0},{4,2},{6,4},{8,6},{10,8},{12,10},{14,12},{16,14},{18,... | collective-permute-start | bytes 31448 | tf_op jit(solution)/shard_map/ppermute | solution.py:29
  390.4 9.5 %collective-permute-start.10 = (f32[1048]{0:T(1024)S(1)}, f32[1048]{0:T(1024)S(1)}, u32[]{:S(2)}, u32[]{:S(2)}) collective-permute-start(f32[1048]{0:T(1024)S(1)} %pad_maximum_fusion.6), channel_id=1, source_target_pairs={{0,1},{1,0},{2,3},{3,2},{4,5},{5,4},{6,7},{7,6},{8,9},{9,8},{10,11... | collective-permute-start | bytes 12584 | tf_op jit(solution)/shard_map/ppermute | solution.py:29
  397.6 163.5 %copy-start.47 = (f32[128]{0:T(128)S(1)}, f32[128]{0:T(128)}, u32[]{:S(2)}) copy-start(f32[128]{0:T(128)} %param.37) | copy-start | bytes 1540
  400.2 160.0 %collective-permute-start.11 = (f32[1048]{0:T(1024)S(1)}, f32[1048]{0:T(1024)S(1)}, u32[]{:S(2)}, u32[]{:S(2)}) collective-permute-start(f32[1048]{0:T(1024)S(1)} %pad_maximum_fusion.7), channel_id=1, source_target_pairs={{0,1},{1,0},{2,3},{3,2},{4,5},{5,4},{6,7},{7,6},{8,9},{9,8},{10,11... | collective-permute-start | bytes 12584 | tf_op jit(solution)/shard_map/ppermute | solution.py:29
  (7 other events, 7.4 us)
Sparse Core Ops, SparseCore 0:
  90.0 36.4 all-gather.3
  178.4 27.9 all-gather.5
  208.6 51.3 all-gather.7
  286.8 73.0 all-reduce.16
where the time goes:
time: 570 us; the launch traced here: 568 us
  blocking collectives  191 us (34%)
  waiting for transfers between devices  187 us (33%)
  starting transfers between devices  63.7 us (11%)
  local copies, waits for them, and re-layouts  43.6 us (8%)
  matrix products  34.8 us (6%)
  other arithmetic  32.7 us (6%)
  between operations  15.8 us (3%)
    psum x1, blocking collectives, body(): stress = lax.psum(virial_part, ('gx', 'gy'))  153 us
    psum x1, waiting for transfers between devices, body(): harm_total, hidden_total = lax.psum((harm_grad, grad_hidden), 'ch')  60.8 us
    all_gather x1, waiting for transfers between devices, body(): lax.all_gather(mix_weight, 'ch', axis=2, tiled=True)  53.5 us
    all_gather x1, waiting for transfers between devices, body(): piece = lax.all_gather(message, 'ch', axis=2, tiled=True)  32.9 us
    psum x1, blocking collectives, body(): energy = lax.psum(energy_part, 'ch')  26.1 us
    all_gather x1, waiting for transfers between devices, body(): piece = lax.all_gather(adjoint_bf, 'ch', axis=2, tiled=True)  25.9 us
    ppermute x4, starting transfers between devices, padded(): lax.ppermute(lax.slice_in_dim(block, 0, width, axis=dim), axis, backward)  24.5 us
    ppermute x4, starting transfers between devices, from_behind(): lax.ppermute(value, axis, [(i, (i + by) % peers) for i in range(peers)])  23.7 us
  transfers between devices with their start and end apart: 16, of which 9 were waited for; matrix products, arithmetic and copies ran while one was open for 7% of the time, Pallas kernels for 0%

commit v1 on v0

v1 whole, which is shorter than its diff:
```python
import functools
import math

import jax
import jax.numpy as jnp
from jax import lax
from jax.experimental import pallas as pl
from jax.experimental.pallas import tpu as pltpu
from jax.sharding import Mesh, PartitionSpec as P

f32 = jnp.float32
bf16 = jnp.bfloat16
cutoff = 3.2
message_scale = 0.25
degree_bounds = ((0, 1), (1, 4), (4, 9))
HIGHEST = lax.Precision.HIGHEST

ATOMS = 32
NEIGH = 32
EDGES = ATOMS * NEIGH
GROUP = 1024
GROUPS = EDGES // GROUP
PER = GROUP // NEIGH
CH = 128
WIDE = 256
HID = 64
MSG = 9 * ATOMS
PAY = MSG + 16
BACK = MSG + ATOMS
SENT = BACK + 16

VMEM_LIMIT = 48 * 1024 * 1024


def nn(a, b):
    return lax.dot_general(a, b, (((1,), (0,)), ((), ())), preferred_element_type=f32)


def nt(a, b):
    return lax.dot_general(a, b, (((1,), (1,)), ((), ())), preferred_element_type=f32)


def tn(a, b):
    return lax.dot_general(a, b, (((0,), (0,)), ((), ())), preferred_element_type=f32)


def split3(v):
    hi = v.astype(bf16)
    rest = v - hi.astype(f32)
    mid = rest.astype(bf16)
    low = (rest - mid.astype(f32)).astype(bf16)
    return hi, mid, low


def split2(v):
    hi = v.astype(bf16)
    return hi, (v - hi.astype(f32)).astype(bf16)


def stacked(parts):
    return jnp.concatenate([part.astype(f32) for part in parts], axis=0)


def iota(shape, dim):
    return lax.broadcasted_iota(jnp.int32, shape, dim)


def call(kernel, out_shape, scratch=(), us=1.0):
    def run(scalars, *arrays):
        return pl.pallas_call(
            kernel,
            out_shape=out_shape,
            in_specs=[pl.BlockSpec(memory_space=pltpu.SMEM)]
            + [pl.BlockSpec(memory_space=pltpu.VMEM)] * len(arrays),
            out_specs=jax.tree.map(lambda _: pl.BlockSpec(memory_space=pltpu.VMEM), out_shape),
            scratch_shapes=list(scratch),
            cost_estimate=pl.CostEstimate(
                flops=int(us * 1e9), bytes_accessed=1 << 18, transcendentals=0
            ),
            compiler_params=pltpu.CompilerParams(vmem_limit_bytes=VMEM_LIMIT),
        )(scalars, *arrays)

    return run


SP_SPEC = 3 * HID
SP_READ = SP_SPEC + 144
SP_OUT = SP_READ + 16
SP_MIX = SP_OUT + 1024
SP_ROWS = SP_MIX + 3 * 1024


def send_kernel(sc, feat, pos, send):
    tiles = [pos[d, r] for d in range(3) for r in range(4)]
    pick = jnp.where(((iota((8, CH), 1) >> 1) & 7) == iota((8, CH), 0), 1.0, 0.0)
    spread = lax.dot_general(
        jnp.concatenate(tiles, axis=0),
        pick,
        (((1,), (0,)), ((), ())),
        precision=HIGHEST,
        preferred_element_type=f32,
    )
    r8 = iota((8, CH), 0)
    l8 = iota((8, CH), 1)
    here = (l8 < 64) & ((l8 >> 4) == (r8 >> 1)) & ((l8 & 1) == (r8 & 1))
    lines = [
        jnp.sum(jnp.where(here, spread[8 * d : 8 * d + 8], 0.0), axis=0, keepdims=True)
        for d in range(3)
    ]
    row = iota((16, CH), 0)
    rows = jnp.zeros((16, CH), f32)
    for d in range(3):
        for k, part in enumerate(split3(lines[d])):
            rows = jnp.where(row == 3 * k + d, part.astype(f32), rows)
    for c in range(2):
        moved = (rows if c == 0 else pltpu.roll(rows, CH - 16, 1)).astype(bf16)
        for y in range(2):
            send[2 * c + y, 0:48] = feat[16 * c : 16 * c + 48]
            send[2 * c + y, 48:64] = moved


def pack_kernel(sc, rad_out, spec, read, ow, mw, spack):
    spack[SP_OUT:SP_MIX] = ow[...]
    spack[SP_MIX:SP_ROWS] = mw[...]
    spack[0:SP_SPEC] = rad_out[...]
    parts = split3(spec[...])
    for k in range(3):
        spack[SP_SPEC + 48 * k : SP_SPEC + 48 * (k + 1)] = parts[k]
    r0, r1, r2 = split3(read[...])
    rr = iota((16, CH), 0)
    rows = (
        jnp.where(rr == 0, r0.astype(f32), 0.0)
        + jnp.where(rr == 1, r1.astype(f32), 0.0)
        + jnp.where(rr == 2, r2.astype(f32), 0.0)
    )
    spack[SP_READ:SP_OUT] = rows.astype(bf16)


def edge_kernel(sc, recv, out):
    start = pl.multiple_of(32 * sc[0], 16)
    for s in range(4):
        out[s, 0:16] = recv[s, pl.ds(start, 16)]
        out[s, 16:32] = recv[s, 48:64]


def feat_table(recv, xrow, yh):
    halves = []
    for cs in range(2):
        o = 2 * cs + yh
        t = 2 * cs + 1 - yh
        halves.append(
            jnp.concatenate([recv[o, 0:48], recv[t, 0:48], xrow[o, 0:16], xrow[t, 0:16]], axis=0)
        )
    return jnp.concatenate(halves, axis=1)


def pos_table(recv, xrow, c, yh):
    lane = iota((16, CH), 1)

    def turned(value, to):
        first = pltpu.roll(value, to - 32, 1)
        return jnp.where(c == 0, first, pltpu.roll(value, to, 1))

    own = recv[yh, 48:64].astype(f32)
    across = pltpu.roll(recv[1 - yh, 48:64].astype(f32), 48, 1)
    row_own = turned(xrow[yh, 16:32].astype(f32), 96)
    row_across = turned(xrow[1 - yh, 16:32].astype(f32), 112)
    table = jnp.where(
        lane < 48, own, jnp.where(lane < 96, across, jnp.where(lane < 112, row_own, row_across))
    )
    return table.astype(bf16)


def ordered(c, own, other):
    first = jnp.where(c == 0, own, other)
    second = jnp.where(c == 0, other, own)
    return first, second


def own_index(c, start, count):
    atom = (iota((1, count), 1) >> 5) + start
    return ((atom >> 4) + c) * 16 + (atom & 15)


def prep_kernel(sc, meta, spk_o, spk_p, rows_ref, rad_ref, rad_t_ref, vec_ref, cho_ref, tmp):
    c = sc[0]
    start = pl.multiple_of(c * ATOMS, ATOMS)
    mine = meta[pl.ds(start, ATOMS), :]
    codes = mine[:, 0:NEIGH].astype(f32).astype(bf16)
    spread = (iota((NEIGH, EDGES), 0) == (iota((NEIGH, EDGES), 1) & 31)).astype(bf16)
    at_atom = iota((ATOMS, EDGES), 0) == (iota((ATOMS, EDGES), 1) >> 5)
    code = jnp.sum(jnp.where(at_atom, nn(codes, spread), 0.0), axis=0, keepdims=True)
    code = code.astype(jnp.int32)
    counts = mine[:, NEIGH : NEIGH + 1].astype(f32)
    count = jnp.sum(jnp.where(at_atom, counts, 0.0), axis=0, keepdims=True)
    lane = iota((1, EDGES), 1)
    slot = lane & 31
    atom = lane >> 5
    col = (atom >> 1) & 7
    third = (code * 43) >> 8
    step_x = third - 1
    step_y = (code >> 1) - 3 * third - 1
    q = (atom >> 4) + step_x + c
    y = col + step_y
    across = jnp.where((y < 0) | (y > 7), 1, 0)
    inside = (q >= 0) & (q <= 2)
    idx = (
        jnp.where(inside, across * 48 + q * 16, 96 + across * 16) + (y & 7) * 2 + (code & 1)
    )
    rows_ref[0:1] = idx.astype(f32)
    rows_ref[1:2] = jnp.where(slot.astype(f32) < count, message_scale, 0.0)
    rows_ref[2:3] = step_x.astype(f32)
    rows_ref[3:4] = step_y.astype(f32)
    rows_ref[4:8] = jnp.zeros((4, EDGES), f32)
    for degree in range(3):
        rows = slice(degree * HID, (degree + 1) * HID)
        first, second = ordered(c, spk_o[rows].astype(f32), spk_p[rows].astype(f32))
        wide = jnp.concatenate([first, second], axis=1)
        rad_ref[degree] = wide.astype(bf16)
        rad_t_ref[degree] = wide.T.astype(bf16)
    vec = 0.0
    for ref in (spk_o, spk_p):
        vec = vec + nt(ref[SP_READ:SP_OUT], ref[SP_OUT:SP_MIX])
    vec = vec[0:1] + vec[1:2] + vec[2:3]
    tmp[...] = jnp.zeros((16, WIDE), f32)
    for b in range(4):
        parts = split3(vec[:, b * WIDE : (b + 1) * WIDE])
        for k in range(3):
            tmp[3 * b + k : 3 * b + k + 1] = parts[k].astype(f32)
    vec_ref[...] = tmp[...].astype(bf16)
    species = mine[:, NEIGH + 1 : NEIGH + 2]
    whole = []
    for ref in (spk_o, spk_p):
        whole.append(
            sum(ref[SP_SPEC + 48 * k : SP_SPEC + 48 * (k + 1)].astype(f32) for k in (2, 1, 0))
        )
    spec = jnp.concatenate(whole, axis=1)
    for t in range(8):
        value = jnp.zeros((ATOMS, WIDE), f32)
        for s in range(6):
            value = jnp.where(species == s, spec[8 * s + t : 8 * s + t + 1], value)
        cho_ref[t] = value


def forward_kernel(
    sc, recv, xrow, prep, rad_in, rad_t, vec, pay, geo, hid_ref, slope, hot_ref, feat_ref, acc
):
    c = sc[0]
    yh = sc[1]
    idx = prep[0:1].astype(jnp.int32)
    scaled = prep[1:2]
    rows = iota((128, EDGES), 0)
    hot = jnp.where(rows == idx, 1.0, 0.0)
    diff = (hot - jnp.where(rows == own_index(c, 0, EDGES), 1.0, 0.0)).astype(bf16)
    moved = nn(pos_table(recv, xrow, c, yh), diff)
    rel = moved[0:3] + moved[3:6] + moved[6:9]
    rx = prep[2:3] + rel[0:1]
    ry = prep[3:4] + rel[1:2]
    rz = rel[2:3]
    rho = jnp.sqrt(rx * rx + ry * ry + rz * rz + 0.25)
    inv = 1.0 / rho
    ux, uy, uz = rx * inv, ry * inv, rz * inv
    ratio = rho / cutoff
    theta = math.pi * ratio
    gap = 1.0 - ratio * ratio
    env = gap * gap * inv
    turns = (iota((8, 1), 0) + 1).astype(f32) * theta
    sins = jnp.sin(turns)
    geo[0:1] = idx.astype(f32)
    geo[1:2] = scaled
    geo[2:3] = rx
    geo[3:4] = ry
    geo[4:5] = rz
    geo[5:6] = rho
    geo[6:7] = inv
    geo[7:8] = env
    geo[8:16] = sins
    geo[16:24] = jnp.cos(turns)
    basis = sins * env
    r_hi, r_mid, r_lo = split3(rad_in[...])
    b_hi, b_mid, b_lo = split3(basis)
    z = tn(
        stacked((r_hi, r_hi, r_mid, r_hi, r_lo, r_mid)).astype(bf16),
        stacked((b_hi, b_mid, b_hi, b_lo, b_hi, b_mid)).astype(bf16),
    )
    sig = lax.logistic(z)
    hidden = (z * sig).astype(bf16)
    hid_ref[...] = hidden
    slope[...] = sig * (1.0 + z * (1.0 - sig))
    harm = (
        scaled,
        scaled * ux,
        scaled * uy,
        scaled * uz,
        scaled * ux * uy,
        scaled * uy * uz,
        scaled * (1.5 * uz * uz - 0.5),
        scaled * ux * uz,
        scaled * 0.5 * (ux * ux - uy * uy),
    )
    for m in range(9):
        geo[24 + m : 25 + m] = harm[m]
    feat_t = feat_table(recv, xrow, yh).astype(f32).T.astype(bf16)
    block = iota((PER, GROUP), 0) == (iota((PER, GROUP), 1) >> 5)
    hot_b = hot.astype(bf16)
    hot_ref[...] = hot_b
    feat_ref[...] = feat_t
    for g in range(GROUPS):
        at = slice(g * GROUP, (g + 1) * GROUP)
        nb = nn(feat_t, hot_b[:, at])
        hid = hidden[:, at]
        radials = nn(rad_t[...].reshape(3 * WIDE, HID), hid)
        for degree, (first, last) in enumerate(degree_bounds):
            p_hi, p_lo = split2(radials[degree * WIDE : (degree + 1) * WIDE] * nb)
            blocks = [jnp.where(block, harm[m][:, at], 0.0) for m in range(first, last)]
            y_hi, y_lo = split2(jnp.concatenate(blocks, axis=0))
            both = nt(jnp.concatenate([y_hi, y_lo], axis=0), p_hi)
            half = (last - first) * PER
            msg = both[:half] + both[half:] + nt(y_hi, p_lo)
            for k in range(last - first):
                r0 = (first + k) * ATOMS + g * PER
                acc[r0 : r0 + PER] = msg[k * PER : (k + 1) * PER]
    pay[0:MSG] = acc[0:MSG].astype(bf16)
    pay[MSG:PAY] = vec[...]


TOP = 14.0


def level_of(value):
    peak = jnp.max(jnp.max(jnp.abs(value), axis=0, keepdims=True), axis=1, keepdims=True)
    return jnp.clip(jnp.floor(jnp.log2(jnp.maximum(peak, 1e-30))), -100.0, 100.0)


def scale_of(adjp, s, row):
    return jnp.exp2(adjp[s, BACK + row : BACK + row + 1, 0:1] - TOP)


def mix_of(spk_o, spk_p, degree):
    at = slice(SP_MIX + 1024 * degree, SP_MIX + 1024 * (degree + 1))
    return jnp.concatenate([spk_o[at], spk_p[at]], axis=1)


def mix_kernel(sc, full, spk_o, spk_p, cho, out):
    c = sc[0]
    x = sc[2]
    at = (iota((16, WIDE), 0) * 43) >> 7
    tall = jnp.zeros((16, WIDE), f32)
    for s in range(4):
        tall = tall + full[s, MSG:PAY, :].astype(f32)
    vec = jnp.sum(jnp.where(at == x, tall, 0.0), axis=0, keepdims=True)
    vec_o, vec_p = ordered(c, vec[:, 0:CH], vec[:, CH:WIDE])
    vec = jnp.concatenate([vec_o, vec_p], axis=1)
    mixed = []
    for degree, (first, last) in enumerate(degree_bounds):
        rows = slice(first * ATOMS, last * ATOMS)
        lhs = jnp.concatenate([full[s, rows, :] for s in range(4)], axis=1)
        both = nn(lhs, mix_of(spk_o, spk_p, degree))
        for m in range(last - first):
            mixed.append(both[m * ATOMS : (m + 1) * ATOMS])

    chosen = [cho[t] for t in range(8)]
    cen, ax, ay, az, qa, qb, qc, qd, qe = mixed
    vec_sq = ax * ax + ay * ay + az * az
    quad_sq = qa * qa + qb * qb + qc * qc + qd * qd + qe * qe
    up = qe - qc
    down = qe + qc
    cubic = (
        up * ax * ax
        - down * ay * ay
        + 2.0 * qc * az * az
        + 2.0 * (qa * ax * ay + qb * ay * az + qd * ax * az)
    )
    cen_sq = cen * cen
    products = (
        cen * chosen[0]
        + cen_sq * chosen[1]
        + vec_sq * chosen[2]
        + quad_sq * chosen[3]
        + cen_sq * cen * chosen[4]
        + cen * vec_sq * chosen[5]
        + cen * quad_sq * chosen[6]
        + cubic * chosen[7]
    )
    first, second = ordered(c, products[:, 0:CH], products[:, CH:WIDE])
    prod = jnp.concatenate([first, second], axis=1).astype(bf16).astype(f32)
    w = [vec * value for value in chosen]
    a_scale = 2.0 * (w[2] + cen * w[5])
    q_scale = 2.0 * (w[3] + cen * w[6])
    w7 = w[7]
    tw7 = 2.0 * w7
    grads = [
        w[0] + 2.0 * cen * w[1] + 3.0 * cen_sq * w[4] + vec_sq * w[5] + quad_sq * w[6],
        a_scale * ax + tw7 * (up * ax + qa * ay + qd * az),
        a_scale * ay + tw7 * (qa * ax - down * ay + qb * az),
        a_scale * az + tw7 * (2.0 * qc * az + qb * ay + qd * ax),
        q_scale * qa + tw7 * ax * ay,
        q_scale * qb + tw7 * ay * az,
        q_scale * qc + w7 * (2.0 * az * az - ax * ax - ay * ay),
        q_scale * qd + tw7 * ax * az,
        q_scale * qe + w7 * (ax * ax - ay * ay),
    ]
    backs = []
    for degree, (first, last) in enumerate(degree_bounds):
        adj = jnp.concatenate(grads[first:last], axis=0).astype(bf16)
        backs.append(nt(adj, mix_of(spk_o, spk_p, degree)))
    back = jnp.concatenate(backs, axis=0)
    level_back, level_prod = level_of(back), level_of(prod)
    back = back * jnp.exp2(TOP - level_back)
    prod = prod * jnp.exp2(TOP - level_prod)
    row = iota((16, WIDE), 0)
    levels = jnp.where(row == 0, level_back, jnp.where(row == 1, level_prod, 0.0))
    for s in range(4):
        out[s, 0:MSG, :] = back[:, s * WIDE : (s + 1) * WIDE]
        out[s, MSG:BACK, :] = prod
        out[s, BACK:SENT, :] = levels


def backward_kernel(
    sc, hot, feat_t, geo, hidden, slope, rad, rad_t, rad_in, adjp, to_y, main, out
):
    c = sc[0]
    yh = sc[1]
    adjm = adjp[0, 0:MSG, :] * scale_of(adjp, 0, 0)
    for s in range(1, 4):
        adjm = adjm + adjp[s, 0:MSG, :] * scale_of(adjp, s, 0)
    r_hi, r_lo = split2(rad_in[...])
    outer = jnp.concatenate([r_hi, r_hi, r_lo], axis=1)
    order = (iota((8, 1), 0) + 1).astype(f32)
    r8 = iota((8, GROUP), 0)
    rows = iota((128, GROUP), 0)
    block = iota((PER, GROUP), 0) == (iota((PER, GROUP), 1) >> 5)

    def rows_of(x, y, z):
        return jnp.where(r8 == 0, x, jnp.where(r8 == 1, y, jnp.where(r8 == 2, z, 0.0)))

    feats = jnp.zeros((128, WIDE), f32)
    found = jnp.zeros((24, CH + 32), f32)
    for g in range(GROUPS):
        at = slice(g * GROUP, (g + 1) * GROUP)
        hot_g = hot[:, at]
        nb = nn(feat_t[...], hot_g)
        hid = hidden[:, at]
        radials = nn(rad_t[...].reshape(3 * WIDE, HID), hid)
        gh = jnp.zeros((HID, GROUP), f32)
        fb = jnp.zeros((WIDE, GROUP), f32)
        gys = []
        scaled = geo[1:2, at]
        for degree, (first, last) in enumerate(degree_bounds):
            radial = radials[degree * WIDE : (degree + 1) * WIDE]
            prod = (radial * nb).astype(bf16)
            blocks = [jnp.where(block, geo[24 + m : 25 + m, at], 0.0) for m in range(first, last)]
            y_hi, y_lo = split2(jnp.concatenate(blocks, axis=0))
            pieces = [
                adjm[m * ATOMS + g * PER : m * ATOMS + (g + 1) * PER] for m in range(first, last)
            ]
            a_hi, a_lo = split2(jnp.concatenate(pieces, axis=0))
            grad_prod = tn(
                jnp.concatenate([a_hi, a_lo, a_hi], axis=0),
                jnp.concatenate([y_hi, y_hi, y_lo], axis=0),
            )
            both = nn(jnp.concatenate([a_hi, a_lo], axis=0), prod)
            half = (last - first) * PER
            over = both[:half] + both[half:]
            for k in range(last - first):
                part = jnp.where(block, over[k * PER : (k + 1) * PER], 0.0)
                gys.append(scaled * jnp.sum(part, axis=0, keepdims=True))
            gh = gh + nn(rad[degree], (grad_prod * nb).astype(bf16))
            fb = fb + grad_prod * radial
        feats = feats + nt(hot_g, fb.astype(bf16))
        rx, ry, rz = geo[2:3, at], geo[3:4, at], geo[4:5, at]
        rho, inv, env = geo[5:6, at], geo[6:7, at], geo[7:8, at]
        d_hi, d_lo = split2(gh * slope[:, at])
        dbasis = nn(outer, jnp.concatenate([d_hi, d_lo, d_hi], axis=0))
        ratio = rho / cutoff
        gap = 1.0 - ratio * ratio
        by_cos = jnp.sum(dbasis * order * geo[16:24, at], axis=0, keepdims=True)
        by_sin = jnp.sum(dbasis * geo[8:16, at], axis=0, keepdims=True)
        drho = by_cos * (math.pi / cutoff) * env - by_sin * inv * (
            env + (4.0 / cutoff) * ratio * gap
        )
        ux, uy, uz = rx * inv, ry * inv, rz * inv
        gx_ = gys[1] + gys[4] * uy + gys[7] * uz + gys[8] * ux
        gy_ = gys[2] + gys[4] * ux + gys[5] * uz - gys[8] * uy
        gz_ = gys[3] + gys[5] * uy + 3.0 * gys[6] * uz + gys[7] * ux
        along = drho - (gx_ * ux + gy_ * uy + gz_ * uz) * inv
        eg = rows_of(gx_ * inv + ux * along, gy_ * inv + uy * along, gz_ * inv + uz * along)
        diff = jnp.where(rows == own_index(c, g * PER, GROUP), 1.0, 0.0) - hot_g.astype(f32)
        places = stacked(split3(rows_of(rx, ry, rz)) + (jnp.zeros((8, GROUP), f32),))
        against = jnp.concatenate([diff, places], axis=0).astype(bf16)
        found = found + nt(stacked(split3(eg)).astype(bf16), against)
    main[0:48] = feats[0:48]
    main[48:64] = feats[96:112]
    to_y[0:48] = feats[48:96].astype(bf16)
    to_y[48:64] = feats[112:128].astype(bf16)
    found = found[0:8] + found[8:16] + found[16:24]
    force = found[:, 0:CH]
    lane = iota((1, CH), 1)
    cross = jnp.concatenate([found[:, CH : CH + 32], jnp.zeros((8, CH - 32), f32)], axis=1)
    cross = cross + pltpu.roll(cross, CH - 8, 1) + pltpu.roll(cross, CH - 16, 1)
    virial = jnp.zeros((1, CH), f32)
    for a in range(3):
        for b in range(3):
            to = 64 + 3 * a + b
            virial = jnp.where(lane == to, pltpu.roll(cross, to - a, 1)[b : b + 1], virial)

    def placed(first, count, to):
        moved = force if to == first else pltpu.roll(force, (to - first) % CH, 1)
        return jnp.where((lane >= to) & (lane < to + count), moved, 0.0)

    def by_core(first, count, to_0, to_1):
        return jnp.where(c == 0, placed(first, count, to_0), placed(first, count, to_1))

    own, beside = sc[3], sc[4]
    goals = (
        (2 * own + yh, by_core(0, 48, 0, 16)),
        (2 * own + 1 - yh, by_core(48, 48, 0, 16)),
        (2 * beside + yh, by_core(96, 16, 48, 0)),
        (2 * beside + 1 - yh, by_core(112, 16, 48, 0)),
    )
    row = iota(out.shape, 0)
    odd = (row & 1) == 1
    total = jnp.where(odd, virial, 0.0)
    for device, value in goals:
        upper = value[0:1] + pltpu.roll(value, 64, 1)[1:2]
        chunk = jnp.where(odd, value[2:3], upper)
        total = total + jnp.where((row >> 1) == device, chunk, 0.0)
    out[...] = total


def layer_kernel(sc, recv, adjp, spk_o, spk_p, layer_ref, level_ref):
    c = sc[0]
    yh = sc[1]
    weights = jnp.concatenate([spk_o[SP_OUT:SP_MIX], spk_p[SP_OUT:SP_MIX]], axis=1)
    parts = [adjp[s, MSG:BACK, :] * scale_of(adjp, s, 1) for s in range(4)]
    both = nn(jnp.concatenate(parts, axis=1).astype(bf16), weights)
    first, second = ordered(c, both[:, 0:CH], both[:, CH:WIDE])
    start = pl.multiple_of(c * 16, 16)
    own_feat = jnp.concatenate(
        [recv[2 * cs + yh, pl.ds(start, ATOMS), :].astype(f32) for cs in range(2)], axis=1
    )
    layer = jnp.concatenate([first, second], axis=1) + own_feat
    layer_ref[...] = layer.astype(bf16)
    ra, rb = ordered(
        c, spk_o[SP_READ:SP_OUT].astype(f32), spk_p[SP_READ:SP_OUT].astype(f32)
    )
    read = jnp.concatenate([ra, rb], axis=1)
    read = read[0:1] + read[1:2] + read[2:3]
    energy = jnp.sum(layer * read, axis=1, keepdims=True)
    lane = iota((ATOMS, CH), 1)
    row = iota((ATOMS, CH), 0)
    level = jnp.sum(jnp.where(lane == row + ATOMS * c, energy, 0.0), axis=0, keepdims=True)
    level_ref[...] = jnp.broadcast_to(level, (8, CH))


def merge_kernel(sc, main, from_y, xback, layer, stay, to_core, acc):
    c = sc[0]
    acc[...] = main[0:48] + from_y[0:48].astype(f32)
    at = pl.ds(pl.multiple_of(32 * c, 16), 16)
    acc[at] = acc[at] + xback[...].astype(f32)
    feat_own, feat_other = ordered(c, acc[:, 0:CH], acc[:, CH:WIDE])
    wide = layer[...].astype(f32)
    layer_own, layer_other = ordered(c, wide[:, 0:CH], wide[:, CH:WIDE])
    stay[0:48] = feat_own.astype(bf16)
    stay[48:80] = layer_own.astype(bf16)
    to_core[0:48] = feat_other.astype(bf16)
    to_core[48:80] = layer_other.astype(bf16)


def finish_kernel(sc, stay, from_core, read, layer_out, feat_grad, acc):
    c = sc[0]
    acc[...] = jnp.broadcast_to(read[...], (64, CH))
    mine = pl.ds(pl.multiple_of(16 * c, 16), 48)
    acc[mine] = acc[mine] + stay[0:48].astype(f32)
    other = pl.ds(pl.multiple_of(16 - 16 * c, 16), 48)
    acc[other] = acc[other] + from_core[0:48].astype(f32)
    feat_grad[...] = acc[...].astype(bf16)
    layer_out[pl.ds(pl.multiple_of(ATOMS * c, ATOMS), ATOMS)] = stay[48:80]
    layer_out[pl.ds(pl.multiple_of(ATOMS - ATOMS * c, ATOMS), ATOMS)] = from_core[48:80]


def total_kernel(sc, got, energy, forces, stress, *, atoms):
    tile = got[0]
    for s in range(1, 8):
        tile = tile + got[s]
    upper, lower, level = tile[0:1], tile[1:2], tile[2:3]
    lines = (upper, pltpu.roll(upper, 64, 1), lower, level)
    row = iota((8, CH), 0)
    lane = iota((8, CH), 1)
    here = (lane < 64) & ((lane >> 4) == (row >> 1)) & ((lane & 1) == (row & 1))
    spread = jnp.concatenate([jnp.where(here, line, 0.0) for line in lines], axis=0)
    pick = jnp.where(((iota((CH, CH), 0) >> 1) & 7) == iota((CH, CH), 1), 1.0, 0.0)
    turned = lax.dot_general(
        spread, pick, (((1,), (0,)), ((), ())), precision=HIGHEST, preferred_element_type=f32
    )
    for k in range(3):
        for r in range(4):
            r0 = 8 * k + 2 * r
            forces[k, r] = turned[r0 : r0 + 2, 0:8]
    for r in range(4):
        energy[r] = turned[24 + 2 * r : 26 + 2 * r, 0:8]
    for a in range(3):
        stress[a : a + 1] = pltpu.roll(lower, CH - 64 - 3 * a, 1)[:, 0:3] * (1.0 / atoms)


def body(
    features,
    positions,
    neighbours,
    counts,
    species,
    radial_in,
    radial_out,
    mix_weight,
    species_weight,
    out_weight,
    readout,
):
    gx = lax.axis_size("g")
    every = gx * lax.axis_size("yh")
    c = lax.axis_index("core")
    own = lax.axis_index("g")
    scalars = jnp.stack(
        [c, lax.axis_index("yh"), lax.axis_index("x"), own, (own + 2 * c - 1 + gx) % gx]
    ).astype(jnp.int32)
    meta = jnp.concatenate(
        [neighbours.reshape(64, NEIGH), counts.reshape(64, 1), species.reshape(64, 1)], axis=1
    )
    shape = jax.ShapeDtypeStruct
    send = call(send_kernel, shape((4, 64, CH), bf16))(
        scalars, features.reshape(64, CH), positions.transpose(0, 1, 3, 2)
    )
    recv = lax.all_to_all(send, ("core", "yh"), 0, 0)
    radial_out, species_weight, send = lax.optimization_barrier((radial_out, species_weight, send))
    spack = call(pack_kernel, shape((SP_ROWS, CH), bf16))(
        scalars,
        radial_out.transpose(1, 0, 2).reshape(3 * HID, CH),
        species_weight.reshape(48, CH),
        readout.reshape(1, CH),
        out_weight,
        mix_weight.reshape(3 * 1024, CH),
    )
    swap = [(0, 1), (1, 0)]
    spack_p = lax.ppermute(spack, "core", swap)
    outward = [
        (co * gx + i, (1 - co) * gx + (i - 1 + 2 * co) % gx) for co in range(2) for i in range(gx)
    ]
    edge_row = call(edge_kernel, shape((4, 32, CH), bf16), us=20.0)(scalars, recv)
    xrow = lax.ppermute(edge_row, ("core", "g"), outward)
    prep, rad, rad_t, vec, cho = call(
        prep_kernel,
        (
            shape((8, EDGES), f32),
            shape((3, HID, WIDE), bf16),
            shape((3, WIDE, HID), bf16),
            shape((16, WIDE), bf16),
            shape((8, ATOMS, WIDE), f32),
        ),
        [pltpu.VMEM((16, WIDE), f32)],
    )(scalars, meta, spack, spack_p)
    pay, geo, hidden, slope, hot, feat_t = call(
        forward_kernel,
        (
            shape((PAY, WIDE), bf16),
            shape((40, EDGES), f32),
            shape((HID, EDGES), bf16),
            shape((HID, EDGES), f32),
            shape((128, EDGES), bf16),
            shape((WIDE, 128), bf16),
        ),
        [pltpu.VMEM((MSG, WIDE), f32)],
        us=3.2,
    )(scalars, recv, xrow, prep, radial_in, rad_t, vec)
    full = lax.all_gather(pay, "x")
    back = call(mix_kernel, shape((4, SENT, WIDE), f32), us=1.7)(
        scalars, full, spack, spack_p, cho
    )
    back = lax.optimization_barrier(back.astype(jnp.float16))
    adjp = lax.optimization_barrier(lax.all_to_all(back, "x", 0, 0)).astype(f32)
    to_y, main, leaving = call(
        backward_kernel,
        (
            shape((64, WIDE), bf16),
            shape((64, WIDE), f32),
            shape((2 * every, CH), f32),
        ),
        us=4.5,
    )(scalars, hot, feat_t, geo, hidden, slope, rad, rad_t, radial_in, adjp)
    from_y = lax.ppermute(to_y, "yh", swap)
    xsend = (main[48:64] + from_y[48:64].astype(f32)).astype(bf16)
    xback = lax.ppermute(xsend, ("core", "g"), outward)
    arrived = lax.all_to_all(leaving, ("g", "yh"), 0, 0, tiled=True)
    layer, level = call(layer_kernel, (shape((ATOMS, WIDE), bf16), shape((8, CH), f32)), us=0.5)(
        scalars, recv, adjp, spack, spack_p
    )
    lines = jnp.sum(arrived.reshape(every, 2, CH), axis=0)
    tile = jnp.concatenate([lines, level[0:6]], axis=0)
    small = jnp.broadcast_to(tile[None], (8, 8, CH))
    main, small = lax.optimization_barrier((main, small))
    got = lax.all_to_all(small, ("x", "core"), 0, 0)
    stay, to_core = call(
        merge_kernel,
        (shape((80, CH), bf16), shape((80, CH), bf16)),
        [pltpu.VMEM((48, WIDE), f32)],
        us=0.05,
    )(scalars, main, from_y, xback, layer)
    from_core = lax.ppermute(to_core, "core", swap)
    layer_out, feat_grad = call(
        finish_kernel,
        (shape((64, CH), bf16), shape((64, CH), bf16)),
        [pltpu.VMEM((64, CH), f32)],
        us=0.05,
    )(scalars, stay, from_core, readout.reshape(1, CH))
    energy, forces, stress = call(
        functools.partial(total_kernel, atoms=64 * every),
        (shape((4, 2, 8), f32), shape((3, 4, 2, 8), f32), shape((3, 3), f32)),
    )(scalars, got)
    block = features.shape
    return (
        layer_out.reshape(block),
        energy.transpose(0, 2, 1),
        forces.transpose(0, 1, 3, 2),
        feat_grad.reshape(block),
        stress,
    )


def solution(mesh):
    gx = mesh.shape["gx"]
    parts = Mesh(mesh.devices.reshape(4, 2, gx, 2), ("x", "core", "g", "yh"))
    ch = ("x", "core")
    placed = (
        P("g", "yh", None, ch),
        P(None, "g", "yh", None),
        P("g", "yh", None, None),
        P("g", "yh", None),
        P("g", "yh", None),
        P(),
        P(None, None, ch),
        P(None, None, ch),
        P(None, None, ch),
        P(None, ch),
        P(ch),
    )
    return jax.shard_map(
        body,
        mesh=parts,
        in_specs=placed,
        out_specs=(
            P("g", "yh", None, ch),
            P("g", "yh", None),
            P(None, "g", "yh", None),
            P("g", "yh", None, ch),
            P(),
        ),
        check_vma=False,
    )
```

time: 570 us -> 103 us (0.18)
  the two profiles are of different devices: /device:TPU:8 before, /device:TPU:1 now
where the time goes in v1:
time: 103 us; the launch traced here: 102 us
  starting transfers between devices  52 us (50%)
  blocking collectives  21.1 us (20%)
  Pallas kernels  16.3 us (16%)
  waiting for transfers between devices  7.44 us (7%)
  local copies, waits for them, and re-layouts  3.76 us (4%)
    all_to_all x1, starting transfers between devices, body(): arrived = lax.all_to_all(leaving, ('g', 'yh'), 0, 0, tiled=True)  18.8 us
    pallas_call x11, Pallas kernels, run(): pl.pallas_call(kernel, out_shape=out_shape, in_specs=[pl.BlockSpec(memory...  16.3 us
    all_to_all x1, blocking collectives, body(): adjp = lax.optimization_barrier(lax.all_to_all(back, 'x', 0, 0)).astype(f32)  11 us
    all_to_all x1, starting transfers between devices, body(): recv = lax.all_to_all(send, ('core', 'yh'), 0, 0)  10.1 us
    all_gather x1, blocking collectives, body(): full = lax.all_gather(pay, 'x')  10.1 us
    ppermute x1, starting transfers between devices, body(): from_y = lax.ppermute(to_y, 'yh', swap)  6.83 us
    ppermute x1, starting transfers between devices, body(): xback = lax.ppermute(xsend, ('core', 'g'), outward)  5.22 us
    all_to_all x1, starting transfers between devices, body(): got = lax.all_to_all(small, ('x', 'core'), 0, 0)  5.11 us
  transfers between devices with their start and end apart: 8, of which 3 were waited for; matrix products, arithmetic and copies ran while one was open for 1% of the time, Pallas kernels for 5%

profile of v1, /device:TPU:1, one launch (start us, length us, event | category | flops | bytes accessed | tf_op | source)
XLA Modules:
  0.0 101.9 jit_solution(1835630972955483687)
XLA Ops:
  0.6 0.1 stack.23.sc
  0.7 0.0 copy-start.6
  0.7 0.7 copy-done.6
  1.5 0.0 copy-start.7
  1.5 0.7 copy-done.7
  2.2 0.0 copy-start.2
  2.2 0.0 copy-start.3
  2.2 0.0 copy-start.4
  2.2 0.0 copy-start.9
  2.2 1.4 %shard_map.146 = bf16[4,64,128]{2,1,0:T(8,128)(2,1)} custom-call(s32[5]{0:T(128)S(1)} %stack.23.sc, bf16[64,128]{1,0:T(8,128)(2,1)S(1)} %bitcast.26, f32[3,4,2,8]{3,2,1,0:T(2,128)S(1)} %bitcast.27), custom_call_target="tpu_custom_call" | custom-call | flops 1000000000 | bytes 262144 | tf_op jit(solution)/shard_map/pallas_call | solution.py:70
  3.6 10.1 %all-to-all-start = ((bf16[4,64,128]{2,1,0:T(8,128)(2,1)}), bf16[4,64,128]{2,1,0:T(8,128)(2,1)S(1)}, u32[]{:S(2)}, u32[]{:S(2)}) async-start(bf16[4,64,128]{2,1,0:T(8,128)(2,1)} %shard_map.146), calls=%async_computation | async-start | bytes 131072 | tf_op jit(solution)/shard_map/all_to_all | solution.py:633
  13.7 0.0 copy-done.2
  13.7 0.0 copy-done.3
  13.7 0.0 copy-done.4
  13.7 0.0 copy-done.5
  13.7 0.0 copy-done.9
  13.7 0.0 copy-start.11
  13.8 0.0 copy-start.12
  13.8 0.0 copy-start.10
  13.8 0.6 shard_map.148.spk_o
  14.4 2.0 %collective-permute-start.1 = (bf16[4448,128]{1,0:T(8,128)(2,1)S(1)}, bf16[4448,128]{1,0:T(8,128)(2,1)S(1)}, u32[]{:S(2)}, u32[]{:S(2)}) collective-permute-start(bf16[4448,128]{1,0:T(8,128)(2,1)S(1)} %shard_map.148.spk_o), channel_id=1, source_target_pairs={{0,64},{64,0},{1,65},{65,1},{2,66},{66,2},{3,67},{67,3},{4,68},{68... | collective-permute-start | bytes 3416072 | tf_op jit(solution)/shard_map/ppermute | solution.py:644
  16.4 0.0 copy-done.11
  16.4 0.1 copy.20
  16.5 0.1 reshape.57
  16.6 0.0 copy-done.12
  16.6 0.1 copy.21
  16.7 0.1 reshape.58
  16.7 0.0 copy-done.10
  16.7 0.1 pad_add_fusion.meta
  16.8 4.0 %all-to-all-done.recv = bf16[4,64,128]{2,1,0:T(8,128)(2,1)S(1)} async-done(((bf16[4,64,128]{2,1,0:T(8,128)(2,1)}), bf16[4,64,128]{2,1,0:T(8,128)(2,1)S(1)}, u32[]{:S(2)}, u32[]{:S(2)}) %all-to-all-start) | async-done | bytes 65568 | tf_op jit(solution)/shard_map/all_to_all | solution.py:633
  20.9 0.5 shard_map.147
  21.4 0.0 copy-start.8
  21.4 1.9 %collective-permute-start = (bf16[4,32,128]{2,1,0:T(8,128)(2,1)S(1)}, bf16[4,32,128]{2,1,0:T(8,128)(2,1)S(1)}, u32[]{:S(2)}, u32[]{:S(2)}) collective-permute-start(bf16[4,32,128]{2,1,0:T(8,128)(2,1)S(1)} %shard_map.147), channel_id=1, source_target_pairs={{0,126},{2,64},{4,66},{6,68},{8,70},{10,72},{12,74},{14,76},{16,78... | collective-permute-start | bytes 98312 | tf_op jit(solution)/shard_map/ppermute | solution.py:649
  23.4 0.0 collective-permute-done.1.spk_p
  23.4 0.0 copy-start
  23.4 0.9 shard_map.149
  24.3 2.3 %collective-permute-done.xrow = bf16[4,32,128]{2,1,0:T(8,128)(2,1)S(1)} collective-permute-done((bf16[4,32,128]{2,1,0:T(8,128)(2,1)S(1)}, bf16[4,32,128]{2,1,0:T(8,128)(2,1)S(1)}, u32[]{:S(2)}, u32[]{:S(2)}) %collective-permute-start) | collective-permute-done | bytes 32800 | tf_op jit(solution)/shard_map/ppermute | solution.py:649
  26.7 0.0 copy-done.8
  26.7 3.0 %shard_map.150 = (bf16[304,256]{1,0:T(8,128)(2,1)S(1)}, f32[40,1024]{1,0:T(8,128)S(1)}, bf16[64,1024]{1,0:T(8,128)(2,1)S(1)}, f32[64,1024]{1,0:T(8,128)S(1)}, bf...) custom-call(s32[5]{0:T(128)S(1)} %stack.23.sc, bf16[4,64,128]{2,1,0:T(8,128)(2,1)S(1)} %all-to-all-done.recv, ...), custom_call_target="tpu_custom_call" | custom-call | flops 3200000000 | bytes 262144 | tf_op jit(solution)/shard_map/pallas_call | solution.py:70
  29.6 10.1 %all-gather = bf16[1216,256]{1,0:T(8,128)(2,1)S(1)} all-gather(bf16[304,256]{1,0:T(8,128)(2,1)S(1)} %get-tuple-element.43), channel_id=2, replica_groups=mesh['x'=4,'core'=2,'g'=32,'yh'=2] {'x'}, dimensions={0}, use_global_device_ids=true | all-gather | bytes 778240 | tf_op jit(solution)/shard_map/all_gather | solution.py:674
  39.7 0.0 copy-done
  39.7 1.9 %shard_map.151 = f32[4,336,256]{2,1,0:T(8,128)S(1)} custom-call(s32[5]{0:T(128)S(1)} %stack.23.sc, bf16[4,304,256]{2,1,0:T(8,128)(2,1)S(1)} %bitcast.21, bf16[4448,128]{1,0:T(8,128)(2,1)S(1)} %shard_map.148.spk_o, bf16[4448,128]{1,0:T(8,128)(2,1)S(1)} %collective-permute-done.1.spk_p, f32[8,32,256]{2,1,0:T(8,128)S(1)} %get-tuple-element.44.cho), custom_call_target="tpu_custom_call" | custom-call | flops 1700000000 | bytes 262144 | tf_op jit(solution)/shard_map/pallas_call | solution.py:70
  41.6 0.1 convert_element_type.12
  41.8 11.0 %all_to_all.24 = f16[4,336,256]{2,1,0:T(8,128)(2,1)S(1)} all-to-all(f16[4,336,256]{2,1,0:T(8,128)(2,1)S(1)} %convert_element_type.12), channel_id=1, replica_groups=mesh['x'=4,'core'=2,'g'=32,'yh'=2] {'x'}, dimensions={0} | all-to-all | bytes 1376256 | tf_op jit(solution)/shard_map/all_to_all | solution.py:679
  52.8 0.1 convert_element_type.13.adjp
  52.9 4.0 %shard_map.152 = (bf16[64,256]{1,0:T(8,128)(2,1)S(1)}, f32[64,256]{1,0:T(8,128)S(1)}, f32[128,128]{1,0:T(8,128)}) custom-call(s32[5]{0:T(128)S(1)} %stack.23.sc, bf16[128,1024]{1,0:T(8,128)(2,1)S(1)} %get-tuple-element.37.hot, bf16[256,128]{1,0:T(8,128)(2,1)S(1)} %get-tuple-element.38.feat_t, f32[40,1024]{1,0:T(8,128)S(1)} %get-tuple-element.39.geo, ...), custom_call_target="tpu_custom_call" | custom-call | flops 4499999744 | bytes 262144 | tf_op jit(solution)/shard_map/pallas_call | solution.py:70
  56.9 18.8 %all-to-all-start.2 = ((f32[64,2,128]{2,1,0:T(2,128)}), f32[64,2,128]{2,1,0:T(2,128)S(1)}, u32[]{:S(2)}, u32[]{:S(2)}) async-start(f32[64,2,128]{2,1,0:T(2,128)} %bitcast.14), calls=%async_computation.2 | async-start | bytes 131072 | tf_op jit(solution)/shard_map/all_to_all | solution.py:692
  75.7 6.8 %collective-permute-start.2 = (bf16[64,256]{1,0:T(8,128)(2,1)S(1)}, bf16[64,256]{1,0:T(8,128)(2,1)S(1)}, u32[]{:S(2)}, u32[]{:S(2)}) collective-permute-start(bf16[64,256]{1,0:T(8,128)(2,1)S(1)} %get-tuple-element.49), channel_id=1, source_target_pairs={{0,1},{1,0},{2,3},{3,2},{4,5},{5,4},{6,7},{7,6},{8,9},{9,8},{10,11... | collective-permute-start | bytes 98312 | tf_op jit(solution)/shard_map/ppermute | solution.py:689
  82.5 0.0 copy-start.1
  82.5 1.2 %copy-done.1 = bf16[4448,128]{1,0:T(8,128)(2,1)S(1)} copy-done((bf16[4448,128]{1,0:T(8,128)(2,1)S(1)}, bf16[4448,128]{1,0:T(8,128)(2,1)}, u32[]{:S(2)}) %copy-start.1) | copy-done | bytes 1138712
  83.7 0.9 shard_map.153
  84.6 0.0 collective-permute-done.2.from_y
  84.6 5.2 %collective-permute-start.3 = (bf16[16,256]{1,0:T(8,128)(2,1)S(1)}, bf16[16,256]{1,0:T(8,128)(2,1)S(1)}, u32[]{:S(2)}, u32[]{:S(2)}) collective-permute-start(bf16[16,256]{1,0:T(8,128)(2,1)S(1)} %add_convert_fusion), channel_id=1, source_target_pairs={{0,126},{2,64},{4,66},{6,68},{8,70},{10,72},{12,74},{14,76},{16,78... | collective-permute-start | bytes 24584 | tf_op jit(solution)/shard_map/ppermute | solution.py:691
  89.9 0.0 all-to-all-done.2
  89.9 0.1 reduce_sum.9
  90.0 0.6 broadcast_in_dim.2
  90.6 5.1 %all-to-all-start.3 = ((f32[8,8,128]{2,1,0:T(8,128)}), f32[8,8,128]{2,1,0:T(8,128)S(1)}, u32[]{:S(2)}, u32[]{:S(2)}) async-start(f32[8,8,128]{2,1,0:T(8,128)} %broadcast_in_dim.2), calls=%async_computation.3 | async-start | bytes 65536 | tf_op jit(solution)/shard_map/all_to_all | solution.py:700
  95.7 0.0 collective-permute-done.3.xback
  95.7 0.6 shard_map.154
  96.3 2.0 %collective-permute-start.4 = (bf16[80,128]{1,0:T(8,128)(2,1)S(1)}, bf16[80,128]{1,0:T(8,128)(2,1)S(1)}, u32[]{:S(2)}, u32[]{:S(2)}) collective-permute-start(bf16[80,128]{1,0:T(8,128)(2,1)S(1)} %get-tuple-element.52), channel_id=1, source_target_pairs={{0,64},{64,0},{1,65},{65,1},{2,66},{66,2},{3,67},{67,3},{4,68},{68... | collective-permute-start | bytes 61448 | tf_op jit(solution)/shard_map/ppermute | solution.py:707
  98.3 1.1 %collective-permute-done.4.from_core = bf16[80,128]{1,0:T(8,128)(2,1)S(1)} collective-permute-done((bf16[80,128]{1,0:T(8,128)(2,1)S(1)}, bf16[80,128]{1,0:T(8,128)(2,1)S(1)}, u32[]{:S(2)}, u32[]{:S(2)}) %collective-permute-start.4) | collective-permute-done | bytes 20512 | tf_op jit(solution)/shard_map/ppermute | solution.py:707
  99.3 1.2 %shard_map.155 = (bf16[64,128]{1,0:T(8,128)(2,1)}, bf16[64,128]{1,0:T(8,128)(2,1)}) custom-call(s32[5]{0:T(128)S(1)} %stack.23.sc, bf16[80,128]{1,0:T(8,128)(2,1)S(1)} %get-tuple-element.51.stay, bf16[80,128]{1,0:T(8,128)(2,1)S(1)} %collective-permute-done.4.from_core, f32[1,128]{1,0:T(1,128)S(1)} %bitcast.29), custom_call_target="tpu_custom_call" | custom-call | flops 50000000 | bytes 262144 | tf_op jit(solution)/shard_map/pallas_call | solution.py:70
  100.5 0.0 all-to-all-done.3.got
  100.5 1.4 %shard_map.156 = (f32[4,2,8]{2,1,0:T(2,128)}, f32[3,4,2,8]{3,2,1,0:T(2,128)}, f32[3,3]{1,0:T(4,128)}) custom-call(s32[5]{0:T(128)S(1)} %stack.23.sc, f32[8,8,128]{2,1,0:T(8,128)S(1)} %all-to-all-done.3.got), custom_call_target="tpu_custom_call" | custom-call | flops 1000000000 | bytes 262144 | tf_op jit(solution)/shard_map/pallas_call | solution.py:70
  (3 shorter events, 0.0 us)
Async XLA Ops:
  0.7 0.7 copy-start.6
  1.5 0.7 copy-start.7
  2.2 11.6 %copy-start.2 = (bf16[3,1024,128]{2,1,0:T(8,128)(2,1)S(1)}, bf16[3,1024,128]{2,1,0:T(8,128)(2,1)}, u32[]{:S(2)}) copy-start(bf16[3,1024,128]{2,1,0:T(8,128)(2,1)} %param.18) | copy-start | bytes 2359300
  2.2 11.6 %copy-start.3 = (bf16[1024,128]{1,0:T(8,128)(2,1)S(1)}, bf16[1024,128]{1,0:T(8,128)(2,1)}, u32[]{:S(2)}) copy-start(bf16[1024,128]{1,0:T(8,128)(2,1)} %ow.1) | copy-start | bytes 786436
  2.2 11.6 %copy-start.4 = (bf16[64,3,128]{2,0,1:T(8,128)(2,1)S(1)}, bf16[64,3,128]{2,0,1:T(8,128)(2,1)}, u32[]{:S(2)}) copy-start(bf16[64,3,128]{2,0,1:T(8,128)(2,1)} %param.17) | copy-start | bytes 147460
  2.2 11.6 %copy-start.5 = (f32[6,8,128]{2,1,0:T(8,128)S(1)}, f32[6,8,128]{2,1,0:T(8,128)}, u32[]{:S(2)}) copy-start(f32[6,8,128]{2,1,0:T(8,128)} %param.19) | copy-start | bytes 73732
  2.2 11.6 %copy-start.9 = (f32[128]{0:T(128)S(1)}, f32[128]{0:T(128)}, u32[]{:S(2)}) copy-start(f32[128]{0:T(128)} %param.21) | copy-start | bytes 1540
  3.6 17.3 %all-to-all-start = ((bf16[4,64,128]{2,1,0:T(8,128)(2,1)}), bf16[4,64,128]{2,1,0:T(8,128)(2,1)S(1)}, u32[]{:S(2)}, u32[]{:S(2)}) async-start(bf16[4,64,128]{2,1,0:T(8,128)(2,1)} %shard_map.146), calls=%async_computation | async-start | bytes 131072 | tf_op jit(solution)/shard_map/all_to_all | solution.py:633
  13.7 2.6 %copy-start.11 = (s32[4,8,2]{1,2,0:T(2,128)S(1)}, s32[4,8,2]{1,2,0:T(2,128)}, u32[]{:S(2)}) copy-start(s32[4,8,2]{1,2,0:T(2,128)} %param.14) | copy-start | bytes 772
  13.8 2.8 %copy-start.12 = (s32[4,8,2]{1,2,0:T(2,128)S(1)}, s32[4,8,2]{1,2,0:T(2,128)}, u32[]{:S(2)}) copy-start(s32[4,8,2]{1,2,0:T(2,128)} %param.15) | copy-start | bytes 772
  13.8 3.0 %copy-start.10 = (s32[4,8,2,32]{3,2,1,0:T(2,128)S(1)}, s32[4,8,2,32]{3,2,1,0:T(2,128)}, u32[]{:S(2)}) copy-start(s32[4,8,2,32]{3,2,1,0:T(2,128)} %param.13) | copy-start | bytes 24580
  14.4 9.0 %collective-permute-start.1 = (bf16[4448,128]{1,0:T(8,128)(2,1)S(1)}, bf16[4448,128]{1,0:T(8,128)(2,1)S(1)}, u32[]{:S(2)}, u32[]{:S(2)}) collective-permute-start(bf16[4448,128]{1,0:T(8,128)(2,1)S(1)} %shard_map.148.spk_o), channel_id=1, source_target_pairs={{0,64},{64,0},{1,65},{65,1},{2,66},{66,2},{3,67},{67,3},{4,68},{68... | collective-permute-start | bytes 3416072 | tf_op jit(solution)/shard_map/ppermute | solution.py:644
  21.4 5.2 %copy-start.8 = (f32[8,64]{1,0:T(8,128)S(1)}, f32[8,64]{1,0:T(8,128)}, u32[]{:S(2)}) copy-start(f32[8,64]{1,0:T(8,128)} %rad_in.3) | copy-start | bytes 6148
  21.4 5.2 %collective-permute-start = (bf16[4,32,128]{2,1,0:T(8,128)(2,1)S(1)}, bf16[4,32,128]{2,1,0:T(8,128)(2,1)S(1)}, u32[]{:S(2)}, u32[]{:S(2)}) collective-permute-start(bf16[4,32,128]{2,1,0:T(8,128)(2,1)S(1)} %shard_map.147), channel_id=1, source_target_pairs={{0,126},{2,64},{4,66},{6,68},{8,70},{10,72},{12,74},{14,76},{16,78... | collective-permute-start | bytes 98312 | tf_op jit(solution)/shard_map/ppermute | solution.py:649
  23.4 16.4 %copy-start = (bf16[4448,128]{1,0:T(8,128)(2,1)}, bf16[4448,128]{1,0:T(8,128)(2,1)S(1)}, u32[]{:S(2)}) copy-start(bf16[4448,128]{1,0:T(8,128)(2,1)S(1)} %collective-permute-done.1.spk_p) | copy-start | bytes 3416068
  56.9 33.0 %all-to-all-start.2 = ((f32[64,2,128]{2,1,0:T(2,128)}), f32[64,2,128]{2,1,0:T(2,128)S(1)}, u32[]{:S(2)}, u32[]{:S(2)}) async-start(f32[64,2,128]{2,1,0:T(2,128)} %bitcast.14), calls=%async_computation.2 | async-start | bytes 131072 | tf_op jit(solution)/shard_map/all_to_all | solution.py:692
  75.7 9.0 %collective-permute-start.2 = (bf16[64,256]{1,0:T(8,128)(2,1)S(1)}, bf16[64,256]{1,0:T(8,128)(2,1)S(1)}, u32[]{:S(2)}, u32[]{:S(2)}) collective-permute-start(bf16[64,256]{1,0:T(8,128)(2,1)S(1)} %get-tuple-element.49), channel_id=1, source_target_pairs={{0,1},{1,0},{2,3},{3,2},{4,5},{5,4},{6,7},{7,6},{8,9},{9,8},{10,11... | collective-permute-start | bytes 98312 | tf_op jit(solution)/shard_map/ppermute | solution.py:689
  82.5 1.3 %copy-start.1 = (bf16[4448,128]{1,0:T(8,128)(2,1)S(1)}, bf16[4448,128]{1,0:T(8,128)(2,1)}, u32[]{:S(2)}) copy-start(bf16[4448,128]{1,0:T(8,128)(2,1)} %copy-done) | copy-start | bytes 3416068
  84.6 11.1 %collective-permute-start.3 = (bf16[16,256]{1,0:T(8,128)(2,1)S(1)}, bf16[16,256]{1,0:T(8,128)(2,1)S(1)}, u32[]{:S(2)}, u32[]{:S(2)}) collective-permute-start(bf16[16,256]{1,0:T(8,128)(2,1)S(1)} %add_convert_fusion), channel_id=1, source_target_pairs={{0,126},{2,64},{4,66},{6,68},{8,70},{10,72},{12,74},{14,76},{16,78... | collective-permute-start | bytes 24584 | tf_op jit(solution)/shard_map/ppermute | solution.py:691
  90.6 9.9 %all-to-all-start.3 = ((f32[8,8,128]{2,1,0:T(8,128)}), f32[8,8,128]{2,1,0:T(8,128)S(1)}, u32[]{:S(2)}, u32[]{:S(2)}) async-start(f32[8,8,128]{2,1,0:T(8,128)} %broadcast_in_dim.2), calls=%async_computation.3 | async-start | bytes 65536 | tf_op jit(solution)/shard_map/all_to_all | solution.py:700
  96.3 3.1 %collective-permute-start.4 = (bf16[80,128]{1,0:T(8,128)(2,1)S(1)}, bf16[80,128]{1,0:T(8,128)(2,1)S(1)}, u32[]{:S(2)}, u32[]{:S(2)}) collective-permute-start(bf16[80,128]{1,0:T(8,128)(2,1)S(1)} %get-tuple-element.52), channel_id=1, source_target_pairs={{0,64},{64,0},{1,65},{65,1},{2,66},{66,2},{3,67},{67,3},{4,68},{68... | collective-permute-start | bytes 61448 | tf_op jit(solution)/shard_map/ppermute | solution.py:707

commit v2 on v1

--- a/solution.py
+++ b/solution.py
@@ -29,7 +29,7 @@
 BACK = MSG + ATOMS
 SENT = BACK + 16
 
-VMEM_LIMIT = 48 * 1024 * 1024
+VMEM_LIMIT = 32 * 1024 * 1024
 
 
 def nn(a, b):
@@ -65,19 +65,19 @@
     return lax.broadcasted_iota(jnp.int32, shape, dim)
 
 
-def call(kernel, out_shape, scratch=(), us=1.0):
+def call(kernel, out_shape, scratch=(), us=1.0, space=pltpu.VMEM, limit=VMEM_LIMIT):
     def run(scalars, *arrays):
         return pl.pallas_call(
             kernel,
             out_shape=out_shape,
             in_specs=[pl.BlockSpec(memory_space=pltpu.SMEM)]
-            + [pl.BlockSpec(memory_space=pltpu.VMEM)] * len(arrays),
+            + [pl.BlockSpec(memory_space=space)] * len(arrays),
             out_specs=jax.tree.map(lambda _: pl.BlockSpec(memory_space=pltpu.VMEM), out_shape),
             scratch_shapes=list(scratch),
             cost_estimate=pl.CostEstimate(
                 flops=int(us * 1e9), bytes_accessed=1 << 18, transcendentals=0
             ),
-            compiler_params=pltpu.CompilerParams(vmem_limit_bytes=VMEM_LIMIT),
+            compiler_params=pltpu.CompilerParams(vmem_limit_bytes=limit),
         )(scalars, *arrays)
 
     return run
@@ -90,7 +90,15 @@
 SP_ROWS = SP_MIX + 3 * 1024
 
 
-def send_kernel(sc, feat, pos, send):
+def send_kernel(sc, feat_any, pos_any, send, feat, pos, sems):
+    copies = (
+        pltpu.make_async_copy(feat_any, feat, sems.at[0]),
+        pltpu.make_async_copy(pos_any, pos, sems.at[1]),
+    )
+    for copy in copies:
+        copy.start()
+    for copy in copies:
+        copy.wait()
     tiles = [pos[d, r] for d in range(3) for r in range(4)]
     pick = jnp.where(((iota((8, CH), 1) >> 1) & 7) == iota((8, CH), 0), 1.0, 0.0)
     spread = lax.dot_general(
@@ -182,7 +190,9 @@
     return ((atom >> 4) + c) * 16 + (atom & 15)
 
 
-def prep_kernel(sc, meta, spk_o, spk_p, rows_ref, rad_ref, rad_t_ref, vec_ref, cho_ref, tmp):
+def prep_kernel(
+    sc, meta, spk_o, spk_p, rows_ref, rad_ref, rad_t_ref, vec_ref, cho_ref, ow_ref, read_ref, tmp
+):
     c = sc[0]
     start = pl.multiple_of(c * ATOMS, ATOMS)
     mine = meta[pl.ds(start, ATOMS), :]
@@ -218,6 +228,12 @@
         wide = jnp.concatenate([first, second], axis=1)
         rad_ref[degree] = wide.astype(bf16)
         rad_t_ref[degree] = wide.T.astype(bf16)
+    ow_ref[...] = jnp.concatenate([spk_o[SP_OUT:SP_MIX], spk_p[SP_OUT:SP_MIX]], axis=1)
+    ra, rb = ordered(
+        c, spk_o[SP_READ:SP_OUT].astype(f32), spk_p[SP_READ:SP_OUT].astype(f32)
+    )
+    read = jnp.concatenate([ra, rb], axis=1)
+    read_ref[...] = jnp.broadcast_to(read[0:1] + read[1:2] + read[2:3], (8, WIDE))
     vec = 0.0
     for ref in (spk_o, spk_p):
         vec = vec + nt(ref[SP_READ:SP_OUT], ref[SP_OUT:SP_MIX])
@@ -528,12 +544,11 @@
     out[...] = total
 
 
-def layer_kernel(sc, recv, adjp, spk_o, spk_p, layer_ref, level_ref):
+def layer_kernel(sc, recv, adjp, weights, read, layer_ref, level_ref):
     c = sc[0]
     yh = sc[1]
-    weights = jnp.concatenate([spk_o[SP_OUT:SP_MIX], spk_p[SP_OUT:SP_MIX]], axis=1)
     parts = [adjp[s, MSG:BACK, :] * scale_of(adjp, s, 1) for s in range(4)]
-    both = nn(jnp.concatenate(parts, axis=1).astype(bf16), weights)
+    both = nn(jnp.concatenate(parts, axis=1).astype(bf16), weights[...])
     first, second = ordered(c, both[:, 0:CH], both[:, CH:WIDE])
     start = pl.multiple_of(c * 16, 16)
     own_feat = jnp.concatenate(
@@ -541,12 +556,7 @@
     )
     layer = jnp.concatenate([first, second], axis=1) + own_feat
     layer_ref[...] = layer.astype(bf16)
-    ra, rb = ordered(
-        c, spk_o[SP_READ:SP_OUT].astype(f32), spk_p[SP_READ:SP_OUT].astype(f32)
-    )
-    read = jnp.concatenate([ra, rb], axis=1)
-    read = read[0:1] + read[1:2] + read[2:3]
-    energy = jnp.sum(layer * read, axis=1, keepdims=True)
+    energy = jnp.sum(layer * read[0:1], axis=1, keepdims=True)
     lane = iota((ATOMS, CH), 1)
     row = iota((ATOMS, CH), 0)
     level = jnp.sum(jnp.where(lane == row + ATOMS * c, energy, 0.0), axis=0, keepdims=True)
@@ -567,7 +577,9 @@
     to_core[48:80] = layer_other.astype(bf16)
 
 
-def finish_kernel(sc, stay, from_core, read, layer_out, feat_grad, acc):
+def finish_kernel(
+    sc, stay, from_core, read, got, layer_out, feat_grad, energy, forces, stress, acc, *, atoms
+):
     c = sc[0]
     acc[...] = jnp.broadcast_to(read[...], (64, CH))
     mine = pl.ds(pl.multiple_of(16 * c, 16), 48)
@@ -577,9 +589,6 @@
     feat_grad[...] = acc[...].astype(bf16)
     layer_out[pl.ds(pl.multiple_of(ATOMS * c, ATOMS), ATOMS)] = stay[48:80]
     layer_out[pl.ds(pl.multiple_of(ATOMS - ATOMS * c, ATOMS), ATOMS)] = from_core[48:80]
-
-
-def total_kernel(sc, got, energy, forces, stress, *, atoms):
     tile = got[0]
     for s in range(1, 8):
         tile = tile + got[s]
@@ -627,7 +636,17 @@
         [neighbours.reshape(64, NEIGH), counts.reshape(64, 1), species.reshape(64, 1)], axis=1
     )
     shape = jax.ShapeDtypeStruct
-    send = call(send_kernel, shape((4, 64, CH), bf16))(
+    send = call(
+        send_kernel,
+        shape((4, 64, CH), bf16),
+        [
+            pltpu.VMEM((64, CH), bf16),
+            pltpu.VMEM((3, 4, 2, 8), f32),
+            pltpu.SemaphoreType.DMA((2,)),
+        ],
+        space=pl.ANY,
+        limit=63 * 1024 * 1024,
+    )(
         scalars, features.reshape(64, CH), positions.transpose(0, 1, 3, 2)
     )
     recv = lax.all_to_all(send, ("core", "yh"), 0, 0)
@@ -647,7 +666,7 @@
     ]
     edge_row = call(edge_kernel, shape((4, 32, CH), bf16), us=20.0)(scalars, recv)
     xrow = lax.ppermute(edge_row, ("core", "g"), outward)
-    prep, rad, rad_t, vec, cho = call(
+    prep, rad, rad_t, vec, cho, wide_out, wide_read = call(
         prep_kernel,
         (
             shape((8, EDGES), f32),
@@ -655,6 +674,8 @@
             shape((3, WIDE, HID), bf16),
             shape((16, WIDE), bf16),
             shape((8, ATOMS, WIDE), f32),
+            shape((1024, WIDE), bf16),
+            shape((8, WIDE), f32),
         ),
         [pltpu.VMEM((16, WIDE), f32)],
     )(scalars, meta, spack, spack_p)
@@ -691,7 +712,7 @@
     xback = lax.ppermute(xsend, ("core", "g"), outward)
     arrived = lax.all_to_all(leaving, ("g", "yh"), 0, 0, tiled=True)
     layer, level = call(layer_kernel, (shape((ATOMS, WIDE), bf16), shape((8, CH), f32)), us=0.5)(
-        scalars, recv, adjp, spack, spack_p
+        scalars, recv, adjp, wide_out, wide_read
     )
     lines = jnp.sum(arrived.reshape(every, 2, CH), axis=0)
     tile = jnp.concatenate([lines, level[0:6]], axis=0)
@@ -705,16 +726,18 @@
         us=0.05,
     )(scalars, main, from_y, xback, layer)
     from_core = lax.ppermute(to_core, "core", swap)
-    layer_out, feat_grad = call(
-        finish_kernel,
-        (shape((64, CH), bf16), shape((64, CH), bf16)),
+    layer_out, feat_grad, energy, forces, stress = call(
+        functools.partial(finish_kernel, atoms=64 * every),
+        (
+            shape((64, CH), bf16),
+            shape((64, CH), bf16),
+            shape((4, 2, 8), f32),
+            shape((3, 4, 2, 8), f32),
+            shape((3, 3), f32),
+        ),
         [pltpu.VMEM((64, CH), f32)],
         us=0.05,
-    )(scalars, stay, from_core, readout.reshape(1, CH))
-    energy, forces, stress = call(
-        functools.partial(total_kernel, atoms=64 * every),
-        (shape((4, 2, 8), f32), shape((3, 4, 2, 8), f32), shape((3, 3), f32)),
-    )(scalars, got)
+    )(scalars, stay, from_core, readout.reshape(1, CH), got)
     block = features.shape
     return (
         layer_out.reshape(block),

time: 103 us -> 104 us (level)
  Pallas kernels: 16.3 us -> 17.6 us
  starting transfers between devices: 52 us -> 53.2 us
  local copies, waits for them, and re-layouts: 3.76 us -> 2.64 us
    unnamed x28 -> x22, local copies, waits for them, and re-layouts: 2.92 us -> 1.18 us
    ppermute x1, waiting for transfers between devices: 0.01 us -> 1.3 us  [body(): from_y = lax.ppermute(to_y, 'yh', swap)]
    pallas_call x11 -> x10, Pallas kernels: 16.3 us -> 17.6 us  [run(): pl.pallas_call(kernel, out_shape=out_shape, in_specs=[pl.BlockSpec(memory...]
  transfers between devices with their start and end apart: 8 -> 8, of which waited for: 3 -> 5; matrix products, arithmetic and copies ran while one was open for 1% -> 1% of each run, Pallas kernels for 5% -> 4%
where the time goes in v2:
time: 104 us; the launch traced here: 103 us
  starting transfers between devices  53.2 us (51%)
  blocking collectives  21 us (20%)
  Pallas kernels  17.6 us (17%)
  waiting for transfers between devices  7.36 us (7%)
  local copies, waits for them, and re-layouts  2.64 us (3%)
    all_to_all x1, starting transfers between devices, body(): arrived = lax.all_to_all(leaving, ('g', 'yh'), 0, 0, tiled=True)  18.9 us
    pallas_call x10, Pallas kernels, run(): pl.pallas_call(kernel, out_shape=out_shape, in_specs=[pl.BlockSpec(memory...  17.6 us
    all_to_all x1, blocking collectives, body(): adjp = lax.optimization_barrier(lax.all_to_all(back, 'x', 0, 0)).astype(f32)  10.9 us
    all_to_all x1, starting transfers between devices, body(): recv = lax.all_to_all(send, ('core', 'yh'), 0, 0)  10.1 us
    all_gather x1, blocking collectives, body(): full = lax.all_gather(pay, 'x')  10.1 us
    ppermute x1, starting transfers between devices, body(): from_y = lax.ppermute(to_y, 'yh', swap)  6.83 us
    ppermute x1, starting transfers between devices, body(): xback = lax.ppermute(xsend, ('core', 'g'), outward)  6.12 us
    all_to_all x1, starting transfers between devices, body(): got = lax.all_to_all(small, ('x', 'core'), 0, 0)  4.48 us
  transfers between devices with their start and end apart: 8, of which 5 were waited for; matrix products, arithmetic and copies ran while one was open for 1% of the time, Pallas kernels for 4%

profile of v2, /device:TPU:1, one launch (start us, length us, event | category | flops | bytes accessed | tf_op | source)
XLA Modules:
  0.0 103.0 jit_solution(155345320774977081)
XLA Ops:
  0.6 0.7 stack.23.sc
  1.3 0.0 copy-start
  1.3 0.0 copy-start.1
  1.3 0.0 copy-start.3
  1.3 0.0 copy-start.4
  1.3 0.0 copy-start.6
  1.4 2.4 %shard_map.146 = bf16[4,64,128]{2,1,0:T(8,128)(2,1)} custom-call(s32[5]{0:T(128)} %stack.23.sc, bf16[64,128]{1,0:T(8,128)(2,1)} %bitcast.29, f32[3,4,2,8]{3,2,1,0:T(2,128)} %bitcast.30), custom_call_target="tpu_custom_call" | custom-call | flops 1000000000 | bytes 262144 | tf_op jit(solution)/shard_map/pallas_call | solution.py:70
  3.8 10.1 %all-to-all-start = ((bf16[4,64,128]{2,1,0:T(8,128)(2,1)}), bf16[4,64,128]{2,1,0:T(8,128)(2,1)S(1)}, u32[]{:S(2)}, u32[]{:S(2)}) async-start(bf16[4,64,128]{2,1,0:T(8,128)(2,1)} %shard_map.146), calls=%async_computation | async-start | bytes 131072 | tf_op jit(solution)/shard_map/all_to_all | solution.py:652
  13.9 0.0 copy-done
  13.9 0.0 copy-done.1
  13.9 0.0 copy-done.3
  13.9 0.0 copy-done.4
  13.9 0.0 copy-done.6
  13.9 0.0 copy-start.2
  13.9 0.9 copy-done.2
  14.9 0.0 copy-start.8
  14.9 0.0 copy-start.9
  14.9 0.0 copy-start.7
  14.9 0.6 shard_map.148.spk_o
  15.5 2.0 %collective-permute-start.1 = (bf16[4448,128]{1,0:T(8,128)(2,1)S(1)}, bf16[4448,128]{1,0:T(8,128)(2,1)}, u32[]{:S(2)}, u32[]{:S(2)}) collective-permute-start(bf16[4448,128]{1,0:T(8,128)(2,1)S(1)} %shard_map.148.spk_o), channel_id=1, source_target_pairs={{0,64},{64,0},{1,65},{65,1},{2,66},{66,2},{3,67},{67,3},{4,68},{68... | collective-permute-start | bytes 3416072 | tf_op jit(solution)/shard_map/ppermute | solution.py:663
  17.5 0.0 copy-done.8
  17.5 0.1 copy.20
  17.6 0.1 reshape.57
  17.7 0.0 copy-done.9
  17.7 0.1 copy.21
  17.8 0.1 reshape.58
  17.8 0.0 copy-done.7
  17.9 0.1 pad_add_fusion.meta
  17.9 3.1 %all-to-all-done.recv = bf16[4,64,128]{2,1,0:T(8,128)(2,1)S(1)} async-done(((bf16[4,64,128]{2,1,0:T(8,128)(2,1)}), bf16[4,64,128]{2,1,0:T(8,128)(2,1)S(1)}, u32[]{:S(2)}, u32[]{:S(2)}) %all-to-all-start) | async-done | bytes 65568 | tf_op jit(solution)/shard_map/all_to_all | solution.py:652
  21.1 0.5 shard_map.147
  21.6 0.0 copy-start.5
  21.6 1.9 %collective-permute-start = (bf16[4,32,128]{2,1,0:T(8,128)(2,1)S(1)}, bf16[4,32,128]{2,1,0:T(8,128)(2,1)S(1)}, u32[]{:S(2)}, u32[]{:S(2)}) collective-permute-start(bf16[4,32,128]{2,1,0:T(8,128)(2,1)S(1)} %shard_map.147), channel_id=1, source_target_pairs={{0,126},{2,64},{4,66},{6,68},{8,70},{10,72},{12,74},{14,76},{16,78... | collective-permute-start | bytes 98312 | tf_op jit(solution)/shard_map/ppermute | solution.py:668
  23.6 0.0 collective-permute-done.1.spk_p
  23.6 1.7 %shard_map.149 = (f32[8,1024]{1,0:T(8,128)S(1)}, bf16[3,64,256]{2,1,0:T(8,128)(2,1)S(1)}, bf16[3,256,64]{2,1,0:T(8,128)(2,1)S(1)}, bf16[16,256]{1,0:T(8,128)(2,1...) custom-call(s32[5]{0:T(128)S(1)} %copy-done, ...), custom_call_target="tpu_custom_call" | custom-call | flops 1000000000 | bytes 262144 | tf_op jit(solution)/shard_map/pallas_call | solution.py:70
  25.2 1.6 %collective-permute-done.xrow = bf16[4,32,128]{2,1,0:T(8,128)(2,1)S(1)} collective-permute-done((bf16[4,32,128]{2,1,0:T(8,128)(2,1)S(1)}, bf16[4,32,128]{2,1,0:T(8,128)(2,1)S(1)}, u32[]{:S(2)}, u32[]{:S(2)}) %collective-permute-start) | collective-permute-done | bytes 32800 | tf_op jit(solution)/shard_map/ppermute | solution.py:668
  26.9 0.0 copy-done.5
  26.9 3.0 %shard_map.150 = (bf16[304,256]{1,0:T(8,128)(2,1)S(1)}, f32[40,1024]{1,0:T(8,128)S(1)}, bf16[64,1024]{1,0:T(8,128)(2,1)S(1)}, f32[64,1024]{1,0:T(8,128)S(1)}, bf...) custom-call(s32[5]{0:T(128)S(1)} %copy-done, bf16[4,64,128]{2,1,0:T(8,128)(2,1)S(1)} %all-to-all-done.recv, ...), custom_call_target="tpu_custom_call" | custom-call | flops 3200000000 | bytes 262144 | tf_op jit(solution)/shard_map/pallas_call | solution.py:70
  29.8 10.1 %all-gather = bf16[1216,256]{1,0:T(8,128)(2,1)S(1)} all-gather(bf16[304,256]{1,0:T(8,128)(2,1)S(1)} %get-tuple-element.45), channel_id=2, replica_groups=mesh['x'=4,'core'=2,'g'=32,'yh'=2] {'x'}, dimensions={0}, use_global_device_ids=true | all-gather | bytes 778240 | tf_op jit(solution)/shard_map/all_gather | solution.py:695
  39.9 2.6 %shard_map.151 = f32[4,336,256]{2,1,0:T(8,128)S(1)} custom-call(s32[5]{0:T(128)S(1)} %copy-done, bf16[4,304,256]{2,1,0:T(8,128)(2,1)S(1)} %bitcast.21, bf16[4448,128]{1,0:T(8,128)(2,1)S(1)} %shard_map.148.spk_o, bf16[4448,128]{1,0:T(8,128)(2,1)} %collective-permute-done.1.spk_p, f32[8,32,256]{2,1,0:T(8,128)S(1)} %get-tuple-element.46.cho), custom_call_target="tpu_custom_call" | custom-call | flops 1700000000 | bytes 262144 | tf_op jit(solution)/shard_map/pallas_call | solution.py:70
  42.5 0.1 convert_element_type.12
  42.7 10.9 %all_to_all.24 = f16[4,336,256]{2,1,0:T(8,128)(2,1)S(1)} all-to-all(f16[4,336,256]{2,1,0:T(8,128)(2,1)S(1)} %convert_element_type.12), channel_id=1, replica_groups=mesh['x'=4,'core'=2,'g'=32,'yh'=2] {'x'}, dimensions={0} | all-to-all | bytes 1376256 | tf_op jit(solution)/shard_map/all_to_all | solution.py:700
  53.5 0.1 convert_element_type.13.adjp
  53.6 4.0 %shard_map.152 = (bf16[64,256]{1,0:T(8,128)(2,1)S(1)}, f32[64,256]{1,0:T(8,128)S(1)}, f32[128,128]{1,0:T(8,128)}) custom-call(s32[5]{0:T(128)S(1)} %copy-done, bf16[128,1024]{1,0:T(8,128)(2,1)S(1)} %get-tuple-element.39.hot, bf16[256,128]{1,0:T(8,128)(2,1)S(1)} %get-tuple-element.40.feat_t, f32[40,1024]{1,0:T(8,128)S(1)} %get-tuple-element.41.geo, ...), custom_call_target="tpu_custom_call" | custom-call | flops 4499999744 | bytes 262144 | tf_op jit(solution)/shard_map/pallas_call | solution.py:70
  57.6 18.9 %all-to-all-start.2 = ((f32[64,2,128]{2,1,0:T(2,128)}), f32[64,2,128]{2,1,0:T(2,128)S(1)}, u32[]{:S(2)}, u32[]{:S(2)}) async-start(f32[64,2,128]{2,1,0:T(2,128)} %bitcast.14), calls=%async_computation.2 | async-start | bytes 131072 | tf_op jit(solution)/shard_map/all_to_all | solution.py:713
  76.6 6.8 %collective-permute-start.2 = (bf16[64,256]{1,0:T(8,128)(2,1)S(1)}, bf16[64,256]{1,0:T(8,128)(2,1)S(1)}, u32[]{:S(2)}, u32[]{:S(2)}) collective-permute-start(bf16[64,256]{1,0:T(8,128)(2,1)S(1)} %get-tuple-element.53), channel_id=1, source_target_pairs={{0,1},{1,0},{2,3},{3,2},{4,5},{5,4},{6,7},{7,6},{8,9},{9,8},{10,11... | collective-permute-start | bytes 98312 | tf_op jit(solution)/shard_map/ppermute | solution.py:710
  83.4 0.9 shard_map.153
  84.3 1.3 %collective-permute-done.2.from_y = bf16[64,256]{1,0:T(8,128)(2,1)S(1)} collective-permute-done((bf16[64,256]{1,0:T(8,128)(2,1)S(1)}, bf16[64,256]{1,0:T(8,128)(2,1)S(1)}, u32[]{:S(2)}, u32[]{:S(2)}) %collective-permute-start.2) | collective-permute-done | bytes 32800 | tf_op jit(solution)/shard_map/ppermute | solution.py:710
  85.6 6.1 %collective-permute-start.3 = (bf16[16,256]{1,0:T(8,128)(2,1)S(1)}, bf16[16,256]{1,0:T(8,128)(2,1)S(1)}, u32[]{:S(2)}, u32[]{:S(2)}) collective-permute-start(bf16[16,256]{1,0:T(8,128)(2,1)S(1)} %add_convert_fusion), channel_id=1, source_target_pairs={{0,126},{2,64},{4,66},{6,68},{8,70},{10,72},{12,74},{14,76},{16,78... | collective-permute-start | bytes 24584 | tf_op jit(solution)/shard_map/ppermute | solution.py:712
  91.7 0.0 all-to-all-done.2
  91.7 0.1 reduce_sum.9
  91.8 0.6 broadcast_in_dim.2
  92.4 4.5 %all-to-all-start.3 = ((f32[8,8,128]{2,1,0:T(8,128)}), f32[8,8,128]{2,1,0:T(8,128)S(1)}, u32[]{:S(2)}, u32[]{:S(2)}) async-start(f32[8,8,128]{2,1,0:T(8,128)} %broadcast_in_dim.2), calls=%async_computation.3 | async-start | bytes 65536 | tf_op jit(solution)/shard_map/all_to_all | solution.py:721
  96.9 0.0 collective-permute-done.3.xback
  96.9 0.6 shard_map.154
  97.5 2.8 %collective-permute-start.4 = (bf16[80,128]{1,0:T(8,128)(2,1)S(1)}, bf16[80,128]{1,0:T(8,128)(2,1)S(1)}, u32[]{:S(2)}, u32[]{:S(2)}) collective-permute-start(bf16[80,128]{1,0:T(8,128)(2,1)S(1)} %get-tuple-element.56), channel_id=1, source_target_pairs={{0,64},{64,0},{1,65},{65,1},{2,66},{66,2},{3,67},{67,3},{4,68},{68... | collective-permute-start | bytes 61448 | tf_op jit(solution)/shard_map/ppermute | solution.py:728
  100.3 0.8 collective-permute-done.4.from_core
  101.1 0.5 all-to-all-done.3.got
  101.6 1.4 %shard_map.155 = (bf16[64,128]{1,0:T(8,128)(2,1)}, bf16[64,128]{1,0:T(8,128)(2,1)}, f32[4,2,8]{2,1,0:T(2,128)}, f32[3,4,2,8]{3,2,1,0:T(2,128)}, f32[3,3]{1,0:T(4,128)}) custom-call(s32[5]{0:T(128)S(1)} %copy-done, bf16[80,128]{1,0:T(8,128)(2,1)S(1)} %get-tuple-element.55.stay, bf16[80,128]{1,0:T(8,128)(2,1)S(1)} %collective-permute-done.4.from_core, ...), custom_call_target="tpu_custom_call" | custom-call | flops 50000000 | bytes 262144 | tf_op jit(solution)/shard_map/pallas_call | solution.py:70
  (2 shorter events, 0.0 us)
Async XLA Ops:
  1.3 12.6 %copy-start = (s32[5]{0:T(128)S(1)}, s32[5]{0:T(128)}, u32[]{:S(2)}) copy-start(s32[5]{0:T(128)} %stack.23.sc) | copy-start | bytes 64
  1.3 12.6 %copy-start.1 = (bf16[3,1024,128]{2,1,0:T(8,128)(2,1)S(1)}, bf16[3,1024,128]{2,1,0:T(8,128)(2,1)}, u32[]{:S(2)}) copy-start(bf16[3,1024,128]{2,1,0:T(8,128)(2,1)} %param.18) | copy-start | bytes 2359300
  1.3 12.6 %copy-start.3 = (bf16[64,3,128]{2,0,1:T(8,128)(2,1)S(1)}, bf16[64,3,128]{2,0,1:T(8,128)(2,1)}, u32[]{:S(2)}) copy-start(bf16[64,3,128]{2,0,1:T(8,128)(2,1)} %param.17) | copy-start | bytes 147460
  1.3 12.6 %copy-start.4 = (f32[6,8,128]{2,1,0:T(8,128)S(1)}, f32[6,8,128]{2,1,0:T(8,128)}, u32[]{:S(2)}) copy-start(f32[6,8,128]{2,1,0:T(8,128)} %param.19) | copy-start | bytes 73732
  1.3 12.6 %copy-start.6 = (f32[128]{0:T(128)S(1)}, f32[128]{0:T(128)}, u32[]{:S(2)}) copy-start(f32[128]{0:T(128)} %param.21) | copy-start | bytes 1540
  3.8 17.3 %all-to-all-start = ((bf16[4,64,128]{2,1,0:T(8,128)(2,1)}), bf16[4,64,128]{2,1,0:T(8,128)(2,1)S(1)}, u32[]{:S(2)}, u32[]{:S(2)}) async-start(bf16[4,64,128]{2,1,0:T(8,128)(2,1)} %shard_map.146), calls=%async_computation | async-start | bytes 131072 | tf_op jit(solution)/shard_map/all_to_all | solution.py:652
  13.9 1.0 copy-start.2
  14.9 2.6 %copy-start.8 = (s32[4,8,2]{1,2,0:T(2,128)S(1)}, s32[4,8,2]{1,2,0:T(2,128)}, u32[]{:S(2)}) copy-start(s32[4,8,2]{1,2,0:T(2,128)} %param.14) | copy-start | bytes 772
  14.9 2.8 %copy-start.9 = (s32[4,8,2]{1,2,0:T(2,128)S(1)}, s32[4,8,2]{1,2,0:T(2,128)}, u32[]{:S(2)}) copy-start(s32[4,8,2]{1,2,0:T(2,128)} %param.15) | copy-start | bytes 772
  14.9 3.0 %copy-start.7 = (s32[4,8,2,32]{3,2,1,0:T(2,128)S(1)}, s32[4,8,2,32]{3,2,1,0:T(2,128)}, u32[]{:S(2)}) copy-start(s32[4,8,2,32]{3,2,1,0:T(2,128)} %param.13) | copy-start | bytes 24580
  15.5 8.0 %collective-permute-start.1 = (bf16[4448,128]{1,0:T(8,128)(2,1)S(1)}, bf16[4448,128]{1,0:T(8,128)(2,1)}, u32[]{:S(2)}, u32[]{:S(2)}) collective-permute-start(bf16[4448,128]{1,0:T(8,128)(2,1)S(1)} %shard_map.148.spk_o), channel_id=1, source_target_pairs={{0,64},{64,0},{1,65},{65,1},{2,66},{66,2},{3,67},{67,3},{4,68},{68... | collective-permute-start | bytes 3416072 | tf_op jit(solution)/shard_map/ppermute | solution.py:663
  21.6 5.2 %copy-start.5 = (f32[8,64]{1,0:T(8,128)S(1)}, f32[8,64]{1,0:T(8,128)}, u32[]{:S(2)}) copy-start(f32[8,64]{1,0:T(8,128)} %rad_in.3) | copy-start | bytes 6148
  21.6 5.2 %collective-permute-start = (bf16[4,32,128]{2,1,0:T(8,128)(2,1)S(1)}, bf16[4,32,128]{2,1,0:T(8,128)(2,1)S(1)}, u32[]{:S(2)}, u32[]{:S(2)}) collective-permute-start(bf16[4,32,128]{2,1,0:T(8,128)(2,1)S(1)} %shard_map.147), channel_id=1, source_target_pairs={{0,126},{2,64},{4,66},{6,68},{8,70},{10,72},{12,74},{14,76},{16,78... | collective-permute-start | bytes 98312 | tf_op jit(solution)/shard_map/ppermute | solution.py:668
  57.6 34.1 %all-to-all-start.2 = ((f32[64,2,128]{2,1,0:T(2,128)}), f32[64,2,128]{2,1,0:T(2,128)S(1)}, u32[]{:S(2)}, u32[]{:S(2)}) async-start(f32[64,2,128]{2,1,0:T(2,128)} %bitcast.14), calls=%async_computation.2 | async-start | bytes 131072 | tf_op jit(solution)/shard_map/all_to_all | solution.py:713
  76.6 9.0 %collective-permute-start.2 = (bf16[64,256]{1,0:T(8,128)(2,1)S(1)}, bf16[64,256]{1,0:T(8,128)(2,1)S(1)}, u32[]{:S(2)}, u32[]{:S(2)}) collective-permute-start(bf16[64,256]{1,0:T(8,128)(2,1)S(1)} %get-tuple-element.53), channel_id=1, source_target_pairs={{0,1},{1,0},{2,3},{3,2},{4,5},{5,4},{6,7},{7,6},{8,9},{9,8},{10,11... | collective-permute-start | bytes 98312 | tf_op jit(solution)/shard_map/ppermute | solution.py:710
  85.6 11.3 %collective-permute-start.3 = (bf16[16,256]{1,0:T(8,128)(2,1)S(1)}, bf16[16,256]{1,0:T(8,128)(2,1)S(1)}, u32[]{:S(2)}, u32[]{:S(2)}) collective-permute-start(bf16[16,256]{1,0:T(8,128)(2,1)S(1)} %add_convert_fusion), channel_id=1, source_target_pairs={{0,126},{2,64},{4,66},{6,68},{8,70},{10,72},{12,74},{14,76},{16,78... | collective-permute-start | bytes 24584 | tf_op jit(solution)/shard_map/ppermute | solution.py:712
  92.4 9.2 %all-to-all-start.3 = ((f32[8,8,128]{2,1,0:T(8,128)}), f32[8,8,128]{2,1,0:T(8,128)S(1)}, u32[]{:S(2)}, u32[]{:S(2)}) async-start(f32[8,8,128]{2,1,0:T(8,128)} %broadcast_in_dim.2), calls=%async_computation.3 | async-start | bytes 65536 | tf_op jit(solution)/shard_map/all_to_all | solution.py:721
  97.5 3.7 %collective-permute-start.4 = (bf16[80,128]{1,0:T(8,128)(2,1)S(1)}, bf16[80,128]{1,0:T(8,128)(2,1)S(1)}, u32[]{:S(2)}, u32[]{:S(2)}) collective-permute-start(bf16[80,128]{1,0:T(8,128)(2,1)S(1)} %get-tuple-element.56), channel_id=1, source_target_pairs={{0,64},{64,0},{1,65},{65,1},{2,66},{66,2},{3,67},{67,3},{4,68},{68... | collective-permute-start | bytes 61448 | tf_op jit(solution)/shard_map/ppermute | solution.py:728

commit v3 on v2

--- a/solution.py
+++ b/solution.py
@@ -29,7 +29,7 @@
 BACK = MSG + ATOMS
 SENT = BACK + 16
 
-VMEM_LIMIT = 32 * 1024 * 1024
+VMEM_LIMIT = 48 * 1024 * 1024
 
 
 def nn(a, b):
@@ -65,19 +65,19 @@
     return lax.broadcasted_iota(jnp.int32, shape, dim)
 
 
-def call(kernel, out_shape, scratch=(), us=1.0, space=pltpu.VMEM, limit=VMEM_LIMIT):
+def call(kernel, out_shape, scratch=(), us=1.0):
     def run(scalars, *arrays):
         return pl.pallas_call(
             kernel,
             out_shape=out_shape,
             in_specs=[pl.BlockSpec(memory_space=pltpu.SMEM)]
-            + [pl.BlockSpec(memory_space=space)] * len(arrays),
+            + [pl.BlockSpec(memory_space=pltpu.VMEM)] * len(arrays),
             out_specs=jax.tree.map(lambda _: pl.BlockSpec(memory_space=pltpu.VMEM), out_shape),
             scratch_shapes=list(scratch),
             cost_estimate=pl.CostEstimate(
                 flops=int(us * 1e9), bytes_accessed=1 << 18, transcendentals=0
             ),
-            compiler_params=pltpu.CompilerParams(vmem_limit_bytes=limit),
+            compiler_params=pltpu.CompilerParams(vmem_limit_bytes=VMEM_LIMIT),
         )(scalars, *arrays)
 
     return run
@@ -90,15 +90,7 @@
 SP_ROWS = SP_MIX + 3 * 1024
 
 
-def send_kernel(sc, feat_any, pos_any, send, feat, pos, sems):
-    copies = (
-        pltpu.make_async_copy(feat_any, feat, sems.at[0]),
-        pltpu.make_async_copy(pos_any, pos, sems.at[1]),
-    )
-    for copy in copies:
-        copy.start()
-    for copy in copies:
-        copy.wait()
+def send_kernel(sc, feat, pos, send):
     tiles = [pos[d, r] for d in range(3) for r in range(4)]
     pick = jnp.where(((iota((8, CH), 1) >> 1) & 7) == iota((8, CH), 0), 1.0, 0.0)
     spread = lax.dot_general(
@@ -636,17 +628,7 @@
         [neighbours.reshape(64, NEIGH), counts.reshape(64, 1), species.reshape(64, 1)], axis=1
     )
     shape = jax.ShapeDtypeStruct
-    send = call(
-        send_kernel,
-        shape((4, 64, CH), bf16),
-        [
-            pltpu.VMEM((64, CH), bf16),
-            pltpu.VMEM((3, 4, 2, 8), f32),
-            pltpu.SemaphoreType.DMA((2,)),
-        ],
-        space=pl.ANY,
-        limit=63 * 1024 * 1024,
-    )(
+    send = call(send_kernel, shape((4, 64, CH), bf16))(
         scalars, features.reshape(64, CH), positions.transpose(0, 1, 3, 2)
     )
     recv = lax.all_to_all(send, ("core", "yh"), 0, 0)

time: 104 us -> 102 us (0.981)
  Pallas kernels: 17.6 us -> 15.1 us
  waiting for transfers between devices: 7.36 us -> 9.74 us
  starting transfers between devices: 53.2 us -> 52 us
    pallas_call x10, Pallas kernels: 17.6 us -> 15.1 us  [run(): pl.pallas_call(kernel, out_shape=out_shape, in_specs=[pl.BlockSpec(memory...]
where the time goes in v3:
time: 102 us
  starting transfers between devices  52 us (51%)
  blocking collectives  21.1 us (21%)
  Pallas kernels  15.1 us (15%)
  waiting for transfers between devices  9.74 us (10%)
  local copies, waits for them, and re-layouts  2.51 us (2%)
    all_to_all x1, starting transfers between devices, body(): arrived = lax.all_to_all(leaving, ('g', 'yh'), 0, 0, tiled=True)  18.8 us
    pallas_call x10, Pallas kernels, run(): pl.pallas_call(kernel, out_shape=out_shape, in_specs=[pl.BlockSpec(memory...  15.1 us
    all_to_all x1, blocking collectives, body(): adjp = lax.optimization_barrier(lax.all_to_all(back, 'x', 0, 0)).astype(f32)  11 us
    all_to_all x1, starting transfers between devices, body(): recv = lax.all_to_all(send, ('core', 'yh'), 0, 0)  10.1 us
    all_gather x1, blocking collectives, body(): full = lax.all_gather(pay, 'x')  10.1 us
    ppermute x1, starting transfers between devices, body(): from_y = lax.ppermute(to_y, 'yh', swap)  6.83 us
    ppermute x1, starting transfers between devices, body(): xback = lax.ppermute(xsend, ('core', 'g'), outward)  5.28 us
    all_to_all x1, starting transfers between devices, body(): got = lax.all_to_all(small, ('x', 'core'), 0, 0)  5.12 us
  transfers between devices with their start and end apart: 8, of which 5 were waited for; matrix products, arithmetic and copies ran while one was open for 1% of the time, Pallas kernels for 4%

profile of v3, /device:TPU:1, one launch (start us, length us, event | category | flops | bytes accessed | tf_op | source)
XLA Modules:
  0.0 101.8 jit_solution(15349689708638822938)
XLA Ops:
  0.6 0.1 stack.23.sc
  0.7 0.0 copy-start.4
  0.7 0.7 copy-done.4
  1.5 0.0 copy-start.5
  1.5 0.7 copy-done.5
  2.2 0.0 copy-start
  2.2 0.0 copy-start.1
  2.2 0.0 copy-start.2
  2.2 0.0 copy-start.3
  2.2 0.0 copy-start.7
  2.2 1.4 %shard_map.146 = bf16[4,64,128]{2,1,0:T(8,128)(2,1)} custom-call(s32[5]{0:T(128)S(1)} %stack.23.sc, bf16[64,128]{1,0:T(8,128)(2,1)S(1)} %bitcast.26, f32[3,4,2,8]{3,2,1,0:T(2,128)S(1)} %bitcast.27), custom_call_target="tpu_custom_call" | custom-call | flops 1000000000 | bytes 262144 | tf_op jit(solution)/shard_map/pallas_call | solution.py:70
  3.6 10.1 %all-to-all-start = ((bf16[4,64,128]{2,1,0:T(8,128)(2,1)}), bf16[4,64,128]{2,1,0:T(8,128)(2,1)S(1)}, u32[]{:S(2)}, u32[]{:S(2)}) async-start(bf16[4,64,128]{2,1,0:T(8,128)(2,1)} %shard_map.146), calls=%async_computation | async-start | bytes 131072 | tf_op jit(solution)/shard_map/all_to_all | solution.py:634
  13.7 0.0 copy-done
  13.7 0.0 copy-done.1
  13.7 0.0 copy-done.2
  13.7 0.0 copy-done.3
  13.7 0.0 copy-done.7
  13.7 0.0 copy-start.9
  13.7 0.0 copy-start.10
  13.8 0.0 copy-start.8
  13.8 0.6 shard_map.148.spk_o
  14.4 2.0 %collective-permute-start.1 = (bf16[4448,128]{1,0:T(8,128)(2,1)S(1)}, bf16[4448,128]{1,0:T(8,128)(2,1)S(1)}, u32[]{:S(2)}, u32[]{:S(2)}) collective-permute-start(bf16[4448,128]{1,0:T(8,128)(2,1)S(1)} %shard_map.148.spk_o), channel_id=1, source_target_pairs={{0,64},{64,0},{1,65},{65,1},{2,66},{66,2},{3,67},{67,3},{4,68},{68... | collective-permute-start | bytes 3416072 | tf_op jit(solution)/shard_map/ppermute | solution.py:645
  16.4 0.0 copy-done.9
  16.4 0.1 copy.20
  16.5 0.1 reshape.57
  16.6 0.0 copy-done.10
  16.6 0.1 copy.21
  16.7 0.1 reshape.58
  16.7 0.0 copy-done.8
  16.7 0.1 pad_add_fusion.meta
  16.8 4.0 %all-to-all-done.recv = bf16[4,64,128]{2,1,0:T(8,128)(2,1)S(1)} async-done(((bf16[4,64,128]{2,1,0:T(8,128)(2,1)}), bf16[4,64,128]{2,1,0:T(8,128)(2,1)S(1)}, u32[]{:S(2)}, u32[]{:S(2)}) %all-to-all-start) | async-done | bytes 65568 | tf_op jit(solution)/shard_map/all_to_all | solution.py:634
  20.9 0.5 shard_map.147
  21.4 0.0 copy-start.6
  21.4 1.9 %collective-permute-start = (bf16[4,32,128]{2,1,0:T(8,128)(2,1)S(1)}, bf16[4,32,128]{2,1,0:T(8,128)(2,1)S(1)}, u32[]{:S(2)}, u32[]{:S(2)}) collective-permute-start(bf16[4,32,128]{2,1,0:T(8,128)(2,1)S(1)} %shard_map.147), channel_id=1, source_target_pairs={{0,126},{2,64},{4,66},{6,68},{8,70},{10,72},{12,74},{14,76},{16,78... | collective-permute-start | bytes 98312 | tf_op jit(solution)/shard_map/ppermute | solution.py:650
  23.4 0.0 collective-permute-done.1.spk_p
  23.4 1.0 shard_map.149
  24.3 2.3 %collective-permute-done.xrow = bf16[4,32,128]{2,1,0:T(8,128)(2,1)S(1)} collective-permute-done((bf16[4,32,128]{2,1,0:T(8,128)(2,1)S(1)}, bf16[4,32,128]{2,1,0:T(8,128)(2,1)S(1)}, u32[]{:S(2)}, u32[]{:S(2)}) %collective-permute-start) | collective-permute-done | bytes 32800 | tf_op jit(solution)/shard_map/ppermute | solution.py:650
  26.7 0.0 copy-done.6
  26.7 3.0 %shard_map.150 = (bf16[304,256]{1,0:T(8,128)(2,1)S(1)}, f32[40,1024]{1,0:T(8,128)S(1)}, bf16[64,1024]{1,0:T(8,128)(2,1)S(1)}, f32[64,1024]{1,0:T(8,128)S(1)}, bf...) custom-call(s32[5]{0:T(128)S(1)} %stack.23.sc, bf16[4,64,128]{2,1,0:T(8,128)(2,1)S(1)} %all-to-all-done.recv, ...), custom_call_target="tpu_custom_call" | custom-call | flops 3200000000 | bytes 262144 | tf_op jit(solution)/shard_map/pallas_call | solution.py:70
  29.6 10.1 %all-gather = bf16[1216,256]{1,0:T(8,128)(2,1)S(1)} all-gather(bf16[304,256]{1,0:T(8,128)(2,1)S(1)} %get-tuple-element.45), channel_id=2, replica_groups=mesh['x'=4,'core'=2,'g'=32,'yh'=2] {'x'}, dimensions={0}, use_global_device_ids=true | all-gather | bytes 778240 | tf_op jit(solution)/shard_map/all_gather | solution.py:677
  39.7 1.9 %shard_map.151 = f32[4,336,256]{2,1,0:T(8,128)S(1)} custom-call(s32[5]{0:T(128)S(1)} %stack.23.sc, bf16[4,304,256]{2,1,0:T(8,128)(2,1)S(1)} %bitcast.21, bf16[4448,128]{1,0:T(8,128)(2,1)S(1)} %shard_map.148.spk_o, bf16[4448,128]{1,0:T(8,128)(2,1)S(1)} %collective-permute-done.1.spk_p, f32[8,32,256]{2,1,0:T(8,128)S(1)} %get-tuple-element.46.cho), custom_call_target="tpu_custom_call" | custom-call | flops 1700000000 | bytes 262144 | tf_op jit(solution)/shard_map/pallas_call | solution.py:70
  41.6 0.1 convert_element_type.12
  41.7 11.0 %all_to_all.24 = f16[4,336,256]{2,1,0:T(8,128)(2,1)S(1)} all-to-all(f16[4,336,256]{2,1,0:T(8,128)(2,1)S(1)} %convert_element_type.12), channel_id=1, replica_groups=mesh['x'=4,'core'=2,'g'=32,'yh'=2] {'x'}, dimensions={0} | all-to-all | bytes 1376256 | tf_op jit(solution)/shard_map/all_to_all | solution.py:682
  52.8 0.1 convert_element_type.13.adjp
  52.9 4.0 %shard_map.152 = (bf16[64,256]{1,0:T(8,128)(2,1)S(1)}, f32[64,256]{1,0:T(8,128)S(1)}, f32[128,128]{1,0:T(8,128)}) custom-call(s32[5]{0:T(128)S(1)} %stack.23.sc, bf16[128,1024]{1,0:T(8,128)(2,1)S(1)} %get-tuple-element.39.hot, bf16[256,128]{1,0:T(8,128)(2,1)S(1)} %get-tuple-element.40.feat_t, f32[40,1024]{1,0:T(8,128)S(1)} %get-tuple-element.41.geo, ...), custom_call_target="tpu_custom_call" | custom-call | flops 4499999744 | bytes 262144 | tf_op jit(solution)/shard_map/pallas_call | solution.py:70
  56.8 18.8 %all-to-all-start.2 = ((f32[64,2,128]{2,1,0:T(2,128)}), f32[64,2,128]{2,1,0:T(2,128)S(1)}, u32[]{:S(2)}, u32[]{:S(2)}) async-start(f32[64,2,128]{2,1,0:T(2,128)} %bitcast.14), calls=%async_computation.2 | async-start | bytes 131072 | tf_op jit(solution)/shard_map/all_to_all | solution.py:695
  75.6 6.8 %collective-permute-start.2 = (bf16[64,256]{1,0:T(8,128)(2,1)S(1)}, bf16[64,256]{1,0:T(8,128)(2,1)S(1)}, u32[]{:S(2)}, u32[]{:S(2)}) collective-permute-start(bf16[64,256]{1,0:T(8,128)(2,1)S(1)} %get-tuple-element.53), channel_id=1, source_target_pairs={{0,1},{1,0},{2,3},{3,2},{4,5},{5,4},{6,7},{7,6},{8,9},{9,8},{10,11... | collective-permute-start | bytes 98312 | tf_op jit(solution)/shard_map/ppermute | solution.py:692
  82.5 0.9 shard_map.153
  83.3 1.2 %collective-permute-done.2.from_y = bf16[64,256]{1,0:T(8,128)(2,1)S(1)} collective-permute-done((bf16[64,256]{1,0:T(8,128)(2,1)S(1)}, bf16[64,256]{1,0:T(8,128)(2,1)S(1)}, u32[]{:S(2)}, u32[]{:S(2)}) %collective-permute-start.2) | collective-permute-done | bytes 32800 | tf_op jit(solution)/shard_map/ppermute | solution.py:692
  84.6 5.3 %collective-permute-start.3 = (bf16[16,256]{1,0:T(8,128)(2,1)S(1)}, bf16[16,256]{1,0:T(8,128)(2,1)S(1)}, u32[]{:S(2)}, u32[]{:S(2)}) collective-permute-start(bf16[16,256]{1,0:T(8,128)(2,1)S(1)} %add_convert_fusion), channel_id=1, source_target_pairs={{0,126},{2,64},{4,66},{6,68},{8,70},{10,72},{12,74},{14,76},{16,78... | collective-permute-start | bytes 24584 | tf_op jit(solution)/shard_map/ppermute | solution.py:694
  89.8 0.0 all-to-all-done.2
  89.9 0.1 reduce_sum.9
  89.9 0.6 broadcast_in_dim.2
  90.6 5.1 %all-to-all-start.3 = ((f32[8,8,128]{2,1,0:T(8,128)}), f32[8,8,128]{2,1,0:T(8,128)S(1)}, u32[]{:S(2)}, u32[]{:S(2)}) async-start(f32[8,8,128]{2,1,0:T(8,128)} %broadcast_in_dim.2), calls=%async_computation.3 | async-start | bytes 65536 | tf_op jit(solution)/shard_map/all_to_all | solution.py:703
  95.7 0.0 collective-permute-done.3.xback
  95.7 0.6 shard_map.154
  96.2 2.0 %collective-permute-start.4 = (bf16[80,128]{1,0:T(8,128)(2,1)S(1)}, bf16[80,128]{1,0:T(8,128)(2,1)S(1)}, u32[]{:S(2)}, u32[]{:S(2)}) collective-permute-start(bf16[80,128]{1,0:T(8,128)(2,1)S(1)} %get-tuple-element.56), channel_id=1, source_target_pairs={{0,64},{64,0},{1,65},{65,1},{2,66},{66,2},{3,67},{67,3},{4,68},{68... | collective-permute-start | bytes 61448 | tf_op jit(solution)/shard_map/ppermute | solution.py:710
  98.3 1.1 %collective-permute-done.4.from_core = bf16[80,128]{1,0:T(8,128)(2,1)S(1)} collective-permute-done((bf16[80,128]{1,0:T(8,128)(2,1)S(1)}, bf16[80,128]{1,0:T(8,128)(2,1)S(1)}, u32[]{:S(2)}, u32[]{:S(2)}) %collective-permute-start.4) | collective-permute-done | bytes 20512 | tf_op jit(solution)/shard_map/ppermute | solution.py:710
  99.3 1.1 %all-to-all-done.3.got = f32[8,8,128]{2,1,0:T(8,128)S(1)} async-done(((f32[8,8,128]{2,1,0:T(8,128)}), f32[8,8,128]{2,1,0:T(8,128)S(1)}, u32[]{:S(2)}, u32[]{:S(2)}) %all-to-all-start.3) | async-done | bytes 32800 | tf_op jit(solution)/shard_map/all_to_all | solution.py:703
  100.4 1.4 %shard_map.155 = (bf16[64,128]{1,0:T(8,128)(2,1)}, bf16[64,128]{1,0:T(8,128)(2,1)}, f32[4,2,8]{2,1,0:T(2,128)}, f32[3,4,2,8]{3,2,1,0:T(2,128)}, f32[3,3]{1,0:T(4,128)}) custom-call(s32[5]{0:T(128)S(1)} %stack.23.sc, bf16[80,128]{1,0:T(8,128)(2,1)S(1)} %get-tuple-element.55.stay, bf16[80,128]{1,0:T(8,128)(2,1)S(1)} %collective-permute-done.4.from_core, ...), custom_call_target="tpu_custom_call" | custom-call | flops 50000000 | bytes 262144 | tf_op jit(solution)/shard_map/pallas_call | solution.py:70
  (2 shorter events, 0.0 us)
Async XLA Ops:
  0.7 0.7 copy-start.4
  1.5 0.7 copy-start.5
  2.2 11.5 %copy-start = (bf16[3,1024,128]{2,1,0:T(8,128)(2,1)S(1)}, bf16[3,1024,128]{2,1,0:T(8,128)(2,1)}, u32[]{:S(2)}) copy-start(bf16[3,1024,128]{2,1,0:T(8,128)(2,1)} %param.18) | copy-start | bytes 2359300
  2.2 11.5 %copy-start.1 = (bf16[1024,128]{1,0:T(8,128)(2,1)S(1)}, bf16[1024,128]{1,0:T(8,128)(2,1)}, u32[]{:S(2)}) copy-start(bf16[1024,128]{1,0:T(8,128)(2,1)} %ow.1) | copy-start | bytes 786436
  2.2 11.6 %copy-start.2 = (bf16[64,3,128]{2,0,1:T(8,128)(2,1)S(1)}, bf16[64,3,128]{2,0,1:T(8,128)(2,1)}, u32[]{:S(2)}) copy-start(bf16[64,3,128]{2,0,1:T(8,128)(2,1)} %param.17) | copy-start | bytes 147460
  2.2 11.6 %copy-start.3 = (f32[6,8,128]{2,1,0:T(8,128)S(1)}, f32[6,8,128]{2,1,0:T(8,128)}, u32[]{:S(2)}) copy-start(f32[6,8,128]{2,1,0:T(8,128)} %param.19) | copy-start | bytes 73732
  2.2 11.6 %copy-start.7 = (f32[128]{0:T(128)S(1)}, f32[128]{0:T(128)}, u32[]{:S(2)}) copy-start(f32[128]{0:T(128)} %param.21) | copy-start | bytes 1540
  3.6 17.3 %all-to-all-start = ((bf16[4,64,128]{2,1,0:T(8,128)(2,1)}), bf16[4,64,128]{2,1,0:T(8,128)(2,1)S(1)}, u32[]{:S(2)}, u32[]{:S(2)}) async-start(bf16[4,64,128]{2,1,0:T(8,128)(2,1)} %shard_map.146), calls=%async_computation | async-start | bytes 131072 | tf_op jit(solution)/shard_map/all_to_all | solution.py:634
  13.7 2.6 %copy-start.9 = (s32[4,8,2]{1,2,0:T(2,128)S(1)}, s32[4,8,2]{1,2,0:T(2,128)}, u32[]{:S(2)}) copy-start(s32[4,8,2]{1,2,0:T(2,128)} %param.14) | copy-start | bytes 772
  13.7 2.8 %copy-start.10 = (s32[4,8,2]{1,2,0:T(2,128)S(1)}, s32[4,8,2]{1,2,0:T(2,128)}, u32[]{:S(2)}) copy-start(s32[4,8,2]{1,2,0:T(2,128)} %param.15) | copy-start | bytes 772
  13.8 3.0 %copy-start.8 = (s32[4,8,2,32]{3,2,1,0:T(2,128)S(1)}, s32[4,8,2,32]{3,2,1,0:T(2,128)}, u32[]{:S(2)}) copy-start(s32[4,8,2,32]{3,2,1,0:T(2,128)} %param.13) | copy-start | bytes 24580
  14.4 9.0 %collective-permute-start.1 = (bf16[4448,128]{1,0:T(8,128)(2,1)S(1)}, bf16[4448,128]{1,0:T(8,128)(2,1)S(1)}, u32[]{:S(2)}, u32[]{:S(2)}) collective-permute-start(bf16[4448,128]{1,0:T(8,128)(2,1)S(1)} %shard_map.148.spk_o), channel_id=1, source_target_pairs={{0,64},{64,0},{1,65},{65,1},{2,66},{66,2},{3,67},{67,3},{4,68},{68... | collective-permute-start | bytes 3416072 | tf_op jit(solution)/shard_map/ppermute | solution.py:645
  21.4 5.2 %copy-start.6 = (f32[8,64]{1,0:T(8,128)S(1)}, f32[8,64]{1,0:T(8,128)}, u32[]{:S(2)}) copy-start(f32[8,64]{1,0:T(8,128)} %rad_in.3) | copy-start | bytes 6148
  21.4 5.2 %collective-permute-start = (bf16[4,32,128]{2,1,0:T(8,128)(2,1)S(1)}, bf16[4,32,128]{2,1,0:T(8,128)(2,1)S(1)}, u32[]{:S(2)}, u32[]{:S(2)}) collective-permute-start(bf16[4,32,128]{2,1,0:T(8,128)(2,1)S(1)} %shard_map.147), channel_id=1, source_target_pairs={{0,126},{2,64},{4,66},{6,68},{8,70},{10,72},{12,74},{14,76},{16,78... | collective-permute-start | bytes 98312 | tf_op jit(solution)/shard_map/ppermute | solution.py:650
  56.8 33.0 %all-to-all-start.2 = ((f32[64,2,128]{2,1,0:T(2,128)}), f32[64,2,128]{2,1,0:T(2,128)S(1)}, u32[]{:S(2)}, u32[]{:S(2)}) async-start(f32[64,2,128]{2,1,0:T(2,128)} %bitcast.14), calls=%async_computation.2 | async-start | bytes 131072 | tf_op jit(solution)/shard_map/all_to_all | solution.py:695
  75.6 8.9 %collective-permute-start.2 = (bf16[64,256]{1,0:T(8,128)(2,1)S(1)}, bf16[64,256]{1,0:T(8,128)(2,1)S(1)}, u32[]{:S(2)}, u32[]{:S(2)}) collective-permute-start(bf16[64,256]{1,0:T(8,128)(2,1)S(1)} %get-tuple-element.53), channel_id=1, source_target_pairs={{0,1},{1,0},{2,3},{3,2},{4,5},{5,4},{6,7},{7,6},{8,9},{9,8},{10,11... | collective-permute-start | bytes 98312 | tf_op jit(solution)/shard_map/ppermute | solution.py:692
  84.6 11.1 %collective-permute-start.3 = (bf16[16,256]{1,0:T(8,128)(2,1)S(1)}, bf16[16,256]{1,0:T(8,128)(2,1)S(1)}, u32[]{:S(2)}, u32[]{:S(2)}) collective-permute-start(bf16[16,256]{1,0:T(8,128)(2,1)S(1)} %add_convert_fusion), channel_id=1, source_target_pairs={{0,126},{2,64},{4,66},{6,68},{8,70},{10,72},{12,74},{14,76},{16,78... | collective-permute-start | bytes 24584 | tf_op jit(solution)/shard_map/ppermute | solution.py:694
  90.6 9.9 %all-to-all-start.3 = ((f32[8,8,128]{2,1,0:T(8,128)}), f32[8,8,128]{2,1,0:T(8,128)S(1)}, u32[]{:S(2)}, u32[]{:S(2)}) async-start(f32[8,8,128]{2,1,0:T(8,128)} %broadcast_in_dim.2), calls=%async_computation.3 | async-start | bytes 65536 | tf_op jit(solution)/shard_map/all_to_all | solution.py:703
  96.2 3.1 %collective-permute-start.4 = (bf16[80,128]{1,0:T(8,128)(2,1)S(1)}, bf16[80,128]{1,0:T(8,128)(2,1)S(1)}, u32[]{:S(2)}, u32[]{:S(2)}) collective-permute-start(bf16[80,128]{1,0:T(8,128)(2,1)S(1)} %get-tuple-element.56), channel_id=1, source_target_pairs={{0,64},{64,0},{1,65},{65,1},{2,66},{66,2},{3,67},{67,3},{4,68},{68... | collective-permute-start | bytes 61448 | tf_op jit(solution)/shard_map/ppermute | solution.py:710

commit v4 on v3

--- a/solution.py
+++ b/solution.py
@@ -183,7 +183,7 @@
 
 
 def prep_kernel(
-    sc, meta, spk_o, spk_p, rows_ref, rad_ref, rad_t_ref, vec_ref, cho_ref, ow_ref, read_ref, tmp
+    sc, meta, spk_o, spk_p, rows_ref, rad_ref, rad_t_ref, vec_ref, cho_ref, ow_ref, read_ref, hot_ref, diff_ref, tmp
 ):
     c = sc[0]
     start = pl.multiple_of(c * ATOMS, ATOMS)
@@ -209,6 +209,10 @@
     idx = (
         jnp.where(inside, across * 48 + q * 16, 96 + across * 16) + (y & 7) * 2 + (code & 1)
     )
+    at_row = iota((128, EDGES), 0)
+    hot = jnp.where(at_row == idx, 1.0, 0.0)
+    hot_ref[...] = hot.astype(bf16)
+    diff_ref[...] = (jnp.where(at_row == own_index(c, 0, EDGES), 1.0, 0.0) - hot).astype(bf16)
     rows_ref[0:1] = idx.astype(f32)
     rows_ref[1:2] = jnp.where(slot.astype(f32) < count, message_scale, 0.0)
     rows_ref[2:3] = step_x.astype(f32)
@@ -251,16 +255,12 @@
 
 
 def forward_kernel(
-    sc, recv, xrow, prep, rad_in, rad_t, vec, pay, geo, hid_ref, slope, hot_ref, feat_ref, acc
+    sc, recv, xrow, prep, hot, diff, rad_in, rad_t, vec, pay, geo, hid_ref, slope, feat_ref, acc
 ):
     c = sc[0]
     yh = sc[1]
-    idx = prep[0:1].astype(jnp.int32)
     scaled = prep[1:2]
-    rows = iota((128, EDGES), 0)
-    hot = jnp.where(rows == idx, 1.0, 0.0)
-    diff = (hot - jnp.where(rows == own_index(c, 0, EDGES), 1.0, 0.0)).astype(bf16)
-    moved = nn(pos_table(recv, xrow, c, yh), diff)
+    moved = -nn(pos_table(recv, xrow, c, yh), diff[...])
     rel = moved[0:3] + moved[3:6] + moved[6:9]
     rx = prep[2:3] + rel[0:1]
     ry = prep[3:4] + rel[1:2]
@@ -274,7 +274,7 @@
     env = gap * gap * inv
     turns = (iota((8, 1), 0) + 1).astype(f32) * theta
     sins = jnp.sin(turns)
-    geo[0:1] = idx.astype(f32)
+    geo[0:1] = scaled
     geo[1:2] = scaled
     geo[2:3] = rx
     geo[3:4] = ry
@@ -310,12 +310,10 @@
         geo[24 + m : 25 + m] = harm[m]
     feat_t = feat_table(recv, xrow, yh).astype(f32).T.astype(bf16)
     block = iota((PER, GROUP), 0) == (iota((PER, GROUP), 1) >> 5)
-    hot_b = hot.astype(bf16)
-    hot_ref[...] = hot_b
     feat_ref[...] = feat_t
     for g in range(GROUPS):
         at = slice(g * GROUP, (g + 1) * GROUP)
-        nb = nn(feat_t, hot_b[:, at])
+        nb = nn(feat_t, hot[:, at])
         hid = hidden[:, at]
         radials = nn(rad_t[...].reshape(3 * WIDE, HID), hid)
         for degree, (first, last) in enumerate(degree_bounds):
@@ -328,8 +326,10 @@
             for k in range(last - first):
                 r0 = (first + k) * ATOMS + g * PER
                 acc[r0 : r0 + PER] = msg[k * PER : (k + 1) * PER]
-    pay[0:MSG] = acc[0:MSG].astype(bf16)
-    pay[MSG:PAY] = vec[...]
+    message = acc[0:MSG].astype(bf16)
+    for s in range(4):
+        pay[s, 0:MSG] = message
+        pay[s, MSG:PAY] = vec[...]
 
 
 TOP = 14.0
@@ -425,7 +425,7 @@
 
 
 def backward_kernel(
-    sc, hot, feat_t, geo, hidden, slope, rad, rad_t, rad_in, adjp, to_y, main, out
+    sc, hot, diff, feat_t, geo, hidden, slope, rad, rad_t, rad_in, adjp, to_y, main, out
 ):
     c = sc[0]
     yh = sc[1]
@@ -436,7 +436,6 @@
     outer = jnp.concatenate([r_hi, r_hi, r_lo], axis=1)
     order = (iota((8, 1), 0) + 1).astype(f32)
     r8 = iota((8, GROUP), 0)
-    rows = iota((128, GROUP), 0)
     block = iota((PER, GROUP), 0) == (iota((PER, GROUP), 1) >> 5)
 
     def rows_of(x, y, z):
@@ -493,9 +492,8 @@
         gz_ = gys[3] + gys[5] * uy + 3.0 * gys[6] * uz + gys[7] * ux
         along = drho - (gx_ * ux + gy_ * uy + gz_ * uz) * inv
         eg = rows_of(gx_ * inv + ux * along, gy_ * inv + uy * along, gz_ * inv + uz * along)
-        diff = jnp.where(rows == own_index(c, g * PER, GROUP), 1.0, 0.0) - hot_g.astype(f32)
         places = stacked(split3(rows_of(rx, ry, rz)) + (jnp.zeros((8, GROUP), f32),))
-        against = jnp.concatenate([diff, places], axis=0).astype(bf16)
+        against = jnp.concatenate([diff[:, at], places.astype(bf16)], axis=0)
         found = found + nt(stacked(split3(eg)).astype(bf16), against)
     main[0:48] = feats[0:48]
     main[48:64] = feats[96:112]
@@ -648,7 +646,7 @@
     ]
     edge_row = call(edge_kernel, shape((4, 32, CH), bf16), us=20.0)(scalars, recv)
     xrow = lax.ppermute(edge_row, ("core", "g"), outward)
-    prep, rad, rad_t, vec, cho, wide_out, wide_read = call(
+    prep, rad, rad_t, vec, cho, wide_out, wide_read, hot, diff = call(
         prep_kernel,
         (
             shape((8, EDGES), f32),
@@ -658,23 +656,24 @@
             shape((8, ATOMS, WIDE), f32),
             shape((1024, WIDE), bf16),
             shape((8, WIDE), f32),
+            shape((128, EDGES), bf16),
+            shape((128, EDGES), bf16),
         ),
         [pltpu.VMEM((16, WIDE), f32)],
     )(scalars, meta, spack, spack_p)
-    pay, geo, hidden, slope, hot, feat_t = call(
+    pay, geo, hidden, slope, feat_t = call(
         forward_kernel,
         (
-            shape((PAY, WIDE), bf16),
+            shape((4, PAY, WIDE), bf16),
             shape((40, EDGES), f32),
             shape((HID, EDGES), bf16),
             shape((HID, EDGES), f32),
-            shape((128, EDGES), bf16),
             shape((WIDE, 128), bf16),
         ),
         [pltpu.VMEM((MSG, WIDE), f32)],
         us=3.2,
-    )(scalars, recv, xrow, prep, radial_in, rad_t, vec)
-    full = lax.all_gather(pay, "x")
+    )(scalars, recv, xrow, prep, hot, diff, radial_in, rad_t, vec)
+    full = lax.all_to_all(pay, "x", 0, 0)
     back = call(mix_kernel, shape((4, SENT, WIDE), f32), us=1.7)(
         scalars, full, spack, spack_p, cho
     )
@@ -688,7 +687,7 @@
             shape((2 * every, CH), f32),
         ),
         us=4.5,
-    )(scalars, hot, feat_t, geo, hidden, slope, rad, rad_t, radial_in, adjp)
+    )(scalars, hot, diff, feat_t, geo, hidden, slope, rad, rad_t, radial_in, adjp)
     from_y = lax.ppermute(to_y, "yh", swap)
     xsend = (main[48:64] + from_y[48:64].astype(f32)).astype(bf16)
     xback = lax.ppermute(xsend, ("core", "g"), outward)

time: 102 us -> 103 us (level)
  starting transfers between devices: 52 us -> 53.2 us
    all_gather x1 -> x0, blocking collectives: 10.1 us -> none  [body(): full = lax.all_gather(pay, 'x')]
    all_to_all x0 -> x1, blocking collectives: none -> 9.85 us  [body(): full = lax.all_to_all(pay, 'x', 0, 0)]
    all_to_all x1, starting transfers between devices: 18.8 us -> 19.9 us  [body(): arrived = lax.all_to_all(leaving, ('g', 'yh'), 0, 0, tiled=True)]
where the time goes in v4:
time: 103 us; the launch traced here: 102 us
  starting transfers between devices  53.2 us (52%)
  blocking collectives  20.3 us (20%)
  Pallas kernels  15.2 us (15%)
  waiting for transfers between devices  9.5 us (9%)
  local copies, waits for them, and re-layouts  2.51 us (2%)
    all_to_all x1, starting transfers between devices, body(): arrived = lax.all_to_all(leaving, ('g', 'yh'), 0, 0, tiled=True)  19.9 us
    pallas_call x10, Pallas kernels, run(): pl.pallas_call(kernel, out_shape=out_shape, in_specs=[pl.BlockSpec(memory...  15.2 us
    all_to_all x1, blocking collectives, body(): adjp = lax.optimization_barrier(lax.all_to_all(back, 'x', 0, 0)).astype(f32)  10.4 us
    all_to_all x1, starting transfers between devices, body(): recv = lax.all_to_all(send, ('core', 'yh'), 0, 0)  10.1 us
    all_to_all x1, blocking collectives, body(): full = lax.all_to_all(pay, 'x', 0, 0)  9.85 us
    ppermute x1, starting transfers between devices, body(): from_y = lax.ppermute(to_y, 'yh', swap)  6.83 us
    all_to_all x1, starting transfers between devices, body(): got = lax.all_to_all(small, ('x', 'core'), 0, 0)  5.85 us
    ppermute x1, starting transfers between devices, body(): xback = lax.ppermute(xsend, ('core', 'g'), outward)  4.6 us
  transfers between devices with their start and end apart: 8, of which 5 were waited for; matrix products, arithmetic and copies ran while one was open for 1% of the time, Pallas kernels for 4%

profile of v4, /device:TPU:1, one launch (start us, length us, event | category | flops | bytes accessed | tf_op | source)
XLA Modules:
  0.0 102.0 jit_solution(10822354204337680126)
XLA Ops:
  0.6 0.1 stack.23.sc
  0.7 0.0 copy-start.4
  0.7 0.7 copy-done.4
  1.5 0.0 copy-start.5
  1.5 0.7 copy-done.5
  2.2 0.0 copy-start
  2.2 0.0 copy-start.1
  2.2 0.0 copy-start.2
  2.2 0.0 copy-start.3
  2.2 0.0 copy-start.7
  2.2 1.4 %shard_map.146 = bf16[4,64,128]{2,1,0:T(8,128)(2,1)} custom-call(s32[5]{0:T(128)S(1)} %stack.23.sc, bf16[64,128]{1,0:T(8,128)(2,1)S(1)} %bitcast.24, f32[3,4,2,8]{3,2,1,0:T(2,128)S(1)} %bitcast.25), custom_call_target="tpu_custom_call" | custom-call | flops 1000000000 | bytes 262144 | tf_op jit(solution)/shard_map/pallas_call | solution.py:70
  3.6 10.1 %all-to-all-start = ((bf16[4,64,128]{2,1,0:T(8,128)(2,1)}), bf16[4,64,128]{2,1,0:T(8,128)(2,1)S(1)}, u32[]{:S(2)}, u32[]{:S(2)}) async-start(bf16[4,64,128]{2,1,0:T(8,128)(2,1)} %shard_map.146), calls=%async_computation | async-start | bytes 131072 | tf_op jit(solution)/shard_map/all_to_all | solution.py:632
  13.7 0.0 copy-done
  13.7 0.0 copy-done.1
  13.7 0.0 copy-done.2
  13.7 0.0 copy-done.3
  13.7 0.0 copy-done.7
  13.7 0.0 copy-start.9
  13.7 0.0 copy-start.10
  13.8 0.0 copy-start.8
  13.8 0.6 shard_map.147.spk_o
  14.4 2.0 %collective-permute-start = (bf16[4448,128]{1,0:T(8,128)(2,1)S(1)}, bf16[4448,128]{1,0:T(8,128)(2,1)S(1)}, u32[]{:S(2)}, u32[]{:S(2)}) collective-permute-start(bf16[4448,128]{1,0:T(8,128)(2,1)S(1)} %shard_map.147.spk_o), channel_id=1, source_target_pairs={{0,64},{64,0},{1,65},{65,1},{2,66},{66,2},{3,67},{67,3},{4,68},{68... | collective-permute-start | bytes 3416072 | tf_op jit(solution)/shard_map/ppermute | solution.py:643
  16.4 0.0 copy-done.9
  16.4 0.1 copy.20
  16.5 0.1 reshape.56
  16.6 0.0 copy-done.10
  16.6 0.1 copy.21
  16.7 0.1 reshape.57
  16.7 0.0 copy-done.8
  16.7 0.1 pad_add_fusion.meta
  16.8 4.0 %all-to-all-done.recv = bf16[4,64,128]{2,1,0:T(8,128)(2,1)S(1)} async-done(((bf16[4,64,128]{2,1,0:T(8,128)(2,1)}), bf16[4,64,128]{2,1,0:T(8,128)(2,1)S(1)}, u32[]{:S(2)}, u32[]{:S(2)}) %all-to-all-start) | async-done | bytes 65568 | tf_op jit(solution)/shard_map/all_to_all | solution.py:632
  20.9 0.5 shard_map.149
  21.4 0.0 copy-start.6
  21.4 1.9 %collective-permute-start.1 = (bf16[4,32,128]{2,1,0:T(8,128)(2,1)S(1)}, bf16[4,32,128]{2,1,0:T(8,128)(2,1)S(1)}, u32[]{:S(2)}, u32[]{:S(2)}) collective-permute-start(bf16[4,32,128]{2,1,0:T(8,128)(2,1)S(1)} %shard_map.149), channel_id=1, source_target_pairs={{0,126},{2,64},{4,66},{6,68},{8,70},{10,72},{12,74},{14,76},{16,78... | collective-permute-start | bytes 98312 | tf_op jit(solution)/shard_map/ppermute | solution.py:648
  23.4 0.0 collective-permute-done.spk_p
  23.4 1.1 %shard_map.148 = (f32[8,1024]{1,0:T(8,128)S(1)}, bf16[3,64,256]{2,1,0:T(8,128)(2,1)S(1)}, bf16[3,256,64]{2,1,0:T(8,128)(2,1)S(1)}, bf16[16,256]{1,0:T(8,128)(2,1...) custom-call(s32[5]{0:T(128)S(1)} %stack.23.sc, ...), custom_call_target="tpu_custom_call" | custom-call | flops 1000000000 | bytes 262144 | tf_op jit(solution)/shard_map/pallas_call | solution.py:70
  24.5 2.2 %collective-permute-done.1.xrow = bf16[4,32,128]{2,1,0:T(8,128)(2,1)S(1)} collective-permute-done((bf16[4,32,128]{2,1,0:T(8,128)(2,1)S(1)}, bf16[4,32,128]{2,1,0:T(8,128)(2,1)S(1)}, u32[]{:S(2)}, u32[]{:S(2)}) %collective-permute-start.1) | collective-permute-done | bytes 32800 | tf_op jit(solution)/shard_map/ppermute | solution.py:648
  26.7 0.0 copy-done.6
  26.7 2.9 %shard_map.150 = (bf16[4,304,256]{2,1,0:T(8,128)(2,1)S(1)}, f32[40,1024]{1,0:T(8,128)S(1)}, bf16[64,1024]{1,0:T(8,128)(2,1)S(1)}, f32[64,1024]{1,0:T(8,128)S(1)}, bf16[256,128]{1,0:T(8,128)(2,1)S(1)}) custom-call(s32[5]{0:T(128)S(1)} %stack.23.sc, bf16[4,64,128]{2,1,0:T(8,128)(2,1)S(1)} %all-to-all-done.recv, ...), custom_call_target="tpu_custom_call" | custom-call | flops 3200000000 | bytes 262144 | tf_op jit(solution)/shard_map/pallas_call | solution.py:70
  29.6 9.9 %all_to_all.29.full = bf16[4,304,256]{2,1,0:T(8,128)(2,1)S(1)} all-to-all(bf16[4,304,256]{2,1,0:T(8,128)(2,1)S(1)} %get-tuple-element.47), channel_id=1, replica_groups=mesh['x'=4,'core'=2,'g'=32,'yh'=2] {'x'}, dimensions={0} | all-to-all | bytes 1245184 | tf_op jit(solution)/shard_map/all_to_all | solution.py:676
  39.4 1.9 %shard_map.151 = f32[4,336,256]{2,1,0:T(8,128)S(1)} custom-call(s32[5]{0:T(128)S(1)} %stack.23.sc, bf16[4,304,256]{2,1,0:T(8,128)(2,1)S(1)} %all_to_all.29.full, bf16[4448,128]{1,0:T(8,128)(2,1)S(1)} %shard_map.147.spk_o, bf16[4448,128]{1,0:T(8,128)(2,1)S(1)} %collective-permute-done.spk_p, f32[8,32,256]{2,1,0:T(8,128)S(1)} %get-tuple-element.48.cho), custom_call_target="tpu_custom_call" | custom-call | flops 1700000000 | bytes 262144 | tf_op jit(solution)/shard_map/pallas_call | solution.py:70
  41.3 0.1 convert_element_type.12
  41.4 10.4 %all_to_all.30 = f16[4,336,256]{2,1,0:T(8,128)(2,1)S(1)} all-to-all(f16[4,336,256]{2,1,0:T(8,128)(2,1)S(1)} %convert_element_type.12), channel_id=1, replica_groups=mesh['x'=4,'core'=2,'g'=32,'yh'=2] {'x'}, dimensions={0} | all-to-all | bytes 1376256 | tf_op jit(solution)/shard_map/all_to_all | solution.py:681
  51.9 0.1 convert_element_type.13.adjp
  52.0 3.9 %shard_map.152 = (bf16[64,256]{1,0:T(8,128)(2,1)S(1)}, f32[64,256]{1,0:T(8,128)S(1)}, f32[128,128]{1,0:T(8,128)}) custom-call(s32[5]{0:T(128)S(1)} %stack.23.sc, bf16[128,1024]{1,0:T(8,128)(2,1)S(1)} %get-tuple-element.37.hot, bf16[128,1024]{1,0:T(8,128)(2,1)S(1)} %get-tuple-element.38.diff, bf16[256,128]{1,0:T(8,128)(2,1)S(1)} %get-tuple-element.42.feat_t, ...), custom_call_target="tpu_custom_call" | custom-call | flops 4499999744 | bytes 262144 | tf_op jit(solution)/shard_map/pallas_call | solution.py:70
  55.9 19.9 %all-to-all-start.3 = ((f32[64,2,128]{2,1,0:T(2,128)}), f32[64,2,128]{2,1,0:T(2,128)S(1)}, u32[]{:S(2)}, u32[]{:S(2)}) async-start(f32[64,2,128]{2,1,0:T(2,128)} %bitcast.13), calls=%async_computation.3 | async-start | bytes 131072 | tf_op jit(solution)/shard_map/all_to_all | solution.py:694
  75.8 6.8 %collective-permute-start.2 = (bf16[64,256]{1,0:T(8,128)(2,1)S(1)}, bf16[64,256]{1,0:T(8,128)(2,1)S(1)}, u32[]{:S(2)}, u32[]{:S(2)}) collective-permute-start(bf16[64,256]{1,0:T(8,128)(2,1)S(1)} %get-tuple-element.55), channel_id=1, source_target_pairs={{0,1},{1,0},{2,3},{3,2},{4,5},{5,4},{6,7},{7,6},{8,9},{9,8},{10,11... | collective-permute-start | bytes 98312 | tf_op jit(solution)/shard_map/ppermute | solution.py:691
  82.7 0.9 shard_map.153
  83.5 1.2 %collective-permute-done.2.from_y = bf16[64,256]{1,0:T(8,128)(2,1)S(1)} collective-permute-done((bf16[64,256]{1,0:T(8,128)(2,1)S(1)}, bf16[64,256]{1,0:T(8,128)(2,1)S(1)}, u32[]{:S(2)}, u32[]{:S(2)}) %collective-permute-start.2) | collective-permute-done | bytes 32800 | tf_op jit(solution)/shard_map/ppermute | solution.py:691
  84.7 4.6 %collective-permute-start.3 = (bf16[16,256]{1,0:T(8,128)(2,1)S(1)}, bf16[16,256]{1,0:T(8,128)(2,1)S(1)}, u32[]{:S(2)}, u32[]{:S(2)}) collective-permute-start(bf16[16,256]{1,0:T(8,128)(2,1)S(1)} %add_convert_fusion), channel_id=1, source_target_pairs={{0,126},{2,64},{4,66},{6,68},{8,70},{10,72},{12,74},{14,76},{16,78... | collective-permute-start | bytes 24584 | tf_op jit(solution)/shard_map/ppermute | solution.py:693
  89.3 0.0 all-to-all-done.3
  89.3 0.1 reduce_sum.9
  89.4 0.6 broadcast_in_dim.2
  90.0 5.9 %all-to-all-start.4 = ((f32[8,8,128]{2,1,0:T(8,128)}), f32[8,8,128]{2,1,0:T(8,128)S(1)}, u32[]{:S(2)}, u32[]{:S(2)}) async-start(f32[8,8,128]{2,1,0:T(8,128)} %broadcast_in_dim.2), calls=%async_computation.4 | async-start | bytes 65536 | tf_op jit(solution)/shard_map/all_to_all | solution.py:702
  95.9 0.0 collective-permute-done.3.xback
  95.9 0.6 shard_map.154
  96.4 2.0 %collective-permute-start.4 = (bf16[80,128]{1,0:T(8,128)(2,1)S(1)}, bf16[80,128]{1,0:T(8,128)(2,1)S(1)}, u32[]{:S(2)}, u32[]{:S(2)}) collective-permute-start(bf16[80,128]{1,0:T(8,128)(2,1)S(1)} %get-tuple-element.58), channel_id=1, source_target_pairs={{0,64},{64,0},{1,65},{65,1},{2,66},{66,2},{3,67},{67,3},{4,68},{68... | collective-permute-start | bytes 61448 | tf_op jit(solution)/shard_map/ppermute | solution.py:709
  98.5 1.1 %collective-permute-done.4.from_core = bf16[80,128]{1,0:T(8,128)(2,1)S(1)} collective-permute-done((bf16[80,128]{1,0:T(8,128)(2,1)S(1)}, bf16[80,128]{1,0:T(8,128)(2,1)S(1)}, u32[]{:S(2)}, u32[]{:S(2)}) %collective-permute-start.4) | collective-permute-done | bytes 20512 | tf_op jit(solution)/shard_map/ppermute | solution.py:709
  99.5 1.1 %all-to-all-done.4.got = f32[8,8,128]{2,1,0:T(8,128)S(1)} async-done(((f32[8,8,128]{2,1,0:T(8,128)}), f32[8,8,128]{2,1,0:T(8,128)S(1)}, u32[]{:S(2)}, u32[]{:S(2)}) %all-to-all-start.4) | async-done | bytes 32800 | tf_op jit(solution)/shard_map/all_to_all | solution.py:702
  100.6 1.4 %shard_map.155 = (bf16[64,128]{1,0:T(8,128)(2,1)}, bf16[64,128]{1,0:T(8,128)(2,1)}, f32[4,2,8]{2,1,0:T(2,128)}, f32[3,4,2,8]{3,2,1,0:T(2,128)}, f32[3,3]{1,0:T(4,128)}) custom-call(s32[5]{0:T(128)S(1)} %stack.23.sc, bf16[80,128]{1,0:T(8,128)(2,1)S(1)} %get-tuple-element.57.stay, bf16[80,128]{1,0:T(8,128)(2,1)S(1)} %collective-permute-done.4.from_core, ...), custom_call_target="tpu_custom_call" | custom-call | flops 50000000 | bytes 262144 | tf_op jit(solution)/shard_map/pallas_call | solution.py:70
  (2 shorter events, 0.0 us)
Async XLA Ops:
  0.7 0.7 copy-start.4
  1.5 0.7 copy-start.5
  2.2 11.5 %copy-start = (bf16[3,1024,128]{2,1,0:T(8,128)(2,1)S(1)}, bf16[3,1024,128]{2,1,0:T(8,128)(2,1)}, u32[]{:S(2)}) copy-start(bf16[3,1024,128]{2,1,0:T(8,128)(2,1)} %param.18) | copy-start | bytes 2359300
  2.2 11.5 %copy-start.1 = (bf16[1024,128]{1,0:T(8,128)(2,1)S(1)}, bf16[1024,128]{1,0:T(8,128)(2,1)}, u32[]{:S(2)}) copy-start(bf16[1024,128]{1,0:T(8,128)(2,1)} %ow.1) | copy-start | bytes 786436
  2.2 11.6 %copy-start.2 = (bf16[64,3,128]{2,0,1:T(8,128)(2,1)S(1)}, bf16[64,3,128]{2,0,1:T(8,128)(2,1)}, u32[]{:S(2)}) copy-start(bf16[64,3,128]{2,0,1:T(8,128)(2,1)} %param.17) | copy-start | bytes 147460
  2.2 11.6 %copy-start.3 = (f32[6,8,128]{2,1,0:T(8,128)S(1)}, f32[6,8,128]{2,1,0:T(8,128)}, u32[]{:S(2)}) copy-start(f32[6,8,128]{2,1,0:T(8,128)} %param.19) | copy-start | bytes 73732
  2.2 11.6 %copy-start.7 = (f32[128]{0:T(128)S(1)}, f32[128]{0:T(128)}, u32[]{:S(2)}) copy-start(f32[128]{0:T(128)} %param.21) | copy-start | bytes 1540
  3.6 17.3 %all-to-all-start = ((bf16[4,64,128]{2,1,0:T(8,128)(2,1)}), bf16[4,64,128]{2,1,0:T(8,128)(2,1)S(1)}, u32[]{:S(2)}, u32[]{:S(2)}) async-start(bf16[4,64,128]{2,1,0:T(8,128)(2,1)} %shard_map.146), calls=%async_computation | async-start | bytes 131072 | tf_op jit(solution)/shard_map/all_to_all | solution.py:632
  13.7 2.6 %copy-start.9 = (s32[4,8,2]{1,2,0:T(2,128)S(1)}, s32[4,8,2]{1,2,0:T(2,128)}, u32[]{:S(2)}) copy-start(s32[4,8,2]{1,2,0:T(2,128)} %param.14) | copy-start | bytes 772
  13.7 2.8 %copy-start.10 = (s32[4,8,2]{1,2,0:T(2,128)S(1)}, s32[4,8,2]{1,2,0:T(2,128)}, u32[]{:S(2)}) copy-start(s32[4,8,2]{1,2,0:T(2,128)} %param.15) | copy-start | bytes 772
  13.8 3.0 %copy-start.8 = (s32[4,8,2,32]{3,2,1,0:T(2,128)S(1)}, s32[4,8,2,32]{3,2,1,0:T(2,128)}, u32[]{:S(2)}) copy-start(s32[4,8,2,32]{3,2,1,0:T(2,128)} %param.13) | copy-start | bytes 24580
  14.4 9.0 %collective-permute-start = (bf16[4448,128]{1,0:T(8,128)(2,1)S(1)}, bf16[4448,128]{1,0:T(8,128)(2,1)S(1)}, u32[]{:S(2)}, u32[]{:S(2)}) collective-permute-start(bf16[4448,128]{1,0:T(8,128)(2,1)S(1)} %shard_map.147.spk_o), channel_id=1, source_target_pairs={{0,64},{64,0},{1,65},{65,1},{2,66},{66,2},{3,67},{67,3},{4,68},{68... | collective-permute-start | bytes 3416072 | tf_op jit(solution)/shard_map/ppermute | solution.py:643
  21.4 5.2 %copy-start.6 = (f32[8,64]{1,0:T(8,128)S(1)}, f32[8,64]{1,0:T(8,128)}, u32[]{:S(2)}) copy-start(f32[8,64]{1,0:T(8,128)} %rad_in.3) | copy-start | bytes 6148
  21.4 5.2 %collective-permute-start.1 = (bf16[4,32,128]{2,1,0:T(8,128)(2,1)S(1)}, bf16[4,32,128]{2,1,0:T(8,128)(2,1)S(1)}, u32[]{:S(2)}, u32[]{:S(2)}) collective-permute-start(bf16[4,32,128]{2,1,0:T(8,128)(2,1)S(1)} %shard_map.149), channel_id=1, source_target_pairs={{0,126},{2,64},{4,66},{6,68},{8,70},{10,72},{12,74},{14,76},{16,78... | collective-permute-start | bytes 98312 | tf_op jit(solution)/shard_map/ppermute | solution.py:648
  55.9 33.4 %all-to-all-start.3 = ((f32[64,2,128]{2,1,0:T(2,128)}), f32[64,2,128]{2,1,0:T(2,128)S(1)}, u32[]{:S(2)}, u32[]{:S(2)}) async-start(f32[64,2,128]{2,1,0:T(2,128)} %bitcast.13), calls=%async_computation.3 | async-start | bytes 131072 | tf_op jit(solution)/shard_map/all_to_all | solution.py:694
  75.8 8.9 %collective-permute-start.2 = (bf16[64,256]{1,0:T(8,128)(2,1)S(1)}, bf16[64,256]{1,0:T(8,128)(2,1)S(1)}, u32[]{:S(2)}, u32[]{:S(2)}) collective-permute-start(bf16[64,256]{1,0:T(8,128)(2,1)S(1)} %get-tuple-element.55), channel_id=1, source_target_pairs={{0,1},{1,0},{2,3},{3,2},{4,5},{5,4},{6,7},{7,6},{8,9},{9,8},{10,11... | collective-permute-start | bytes 98312 | tf_op jit(solution)/shard_map/ppermute | solution.py:691
  84.7 11.2 %collective-permute-start.3 = (bf16[16,256]{1,0:T(8,128)(2,1)S(1)}, bf16[16,256]{1,0:T(8,128)(2,1)S(1)}, u32[]{:S(2)}, u32[]{:S(2)}) collective-permute-start(bf16[16,256]{1,0:T(8,128)(2,1)S(1)} %add_convert_fusion), channel_id=1, source_target_pairs={{0,126},{2,64},{4,66},{6,68},{8,70},{10,72},{12,74},{14,76},{16,78... | collective-permute-start | bytes 24584 | tf_op jit(solution)/shard_map/ppermute | solution.py:693
  90.0 10.6 %all-to-all-start.4 = ((f32[8,8,128]{2,1,0:T(8,128)}), f32[8,8,128]{2,1,0:T(8,128)S(1)}, u32[]{:S(2)}, u32[]{:S(2)}) async-start(f32[8,8,128]{2,1,0:T(8,128)} %broadcast_in_dim.2), calls=%async_computation.4 | async-start | bytes 65536 | tf_op jit(solution)/shard_map/all_to_all | solution.py:702
  96.4 3.1 %collective-permute-start.4 = (bf16[80,128]{1,0:T(8,128)(2,1)S(1)}, bf16[80,128]{1,0:T(8,128)(2,1)S(1)}, u32[]{:S(2)}, u32[]{:S(2)}) collective-permute-start(bf16[80,128]{1,0:T(8,128)(2,1)S(1)} %get-tuple-element.58), channel_id=1, source_target_pairs={{0,64},{64,0},{1,65},{65,1},{2,66},{66,2},{3,67},{67,3},{4,68},{68... | collective-permute-start | bytes 61448 | tf_op jit(solution)/shard_map/ppermute | solution.py:709
